TPU v7x, 32 devices: a whole 2x2x4 slice. The times are simulated.
32 devices in a mesh: expert: 4 (over y, x), context: 2 (over core), dp: 4 (over z).
Axes of the slice: x: 2, y: 2, z: 4, core: 2. Of those that a mesh axis runs over, the one named last changes fastest.
Arguments:
- tokens: bfloat16 [16, 2048, 768], P(('expert', 'dp'), 'context'), may hold values from -6 to 6
- segments: int32 [16, 2048], P(('expert', 'dp'), 'context'), may hold values from 0 to 4, as said below
- routes: int32 [16, 2048, 2], P(('expert', 'dp'), 'context'), may hold values from 0 to 7, all different within a row
- prev_logits: float32 [16, 2048, 8], P(('expert', 'dp'), 'context'), may hold values from -3 to 3
- ranks: int32 [16, 2, 1024], P(('expert', 'dp'), 'context'), may hold values from 0 to 1023, each once within a row
- cotangent: bfloat16 [16, 2048, 768], P(('expert', 'dp'), 'context'), may hold values from -6 to 6
- norm_one: bfloat16 [768], P('dp'), may hold values from 0.099609375 to 1.8984375
- w_query: bfloat16 [768, 768], P('dp'), may hold values from -0.21875 to 0.21875
- w_key: bfloat16 [768, 768], P('dp'), may hold values from -0.21875 to 0.21875
- w_value: bfloat16 [768, 768], P('dp'), may hold values from -0.21875 to 0.21875
- w_out: bfloat16 [768, 768], P('dp'), may hold values from -0.875 to 0.875
- norm_two: bfloat16 [768], P('dp'), may hold values from 0.099609375 to 1.8984375
- router: bfloat16 [768, 8], P('dp'), may hold values from -0.15625 to 0.15625
- w_res: bfloat16 [8, 8], replicated, may hold values from -2 to 2
- const_mix: bfloat16 [768, 4], P('dp'), may hold values from -0.21875 to 0.21875
- const_vec: bfloat16 [768, 2], P('dp'), may hold values from -5 to 5
- w_gate: bfloat16 [4, 768, 2048], P('expert', 'dp'), may hold values from -0.21875 to 0.21875
- w_up: bfloat16 [4, 768, 2048], P('expert', 'dp'), may hold values from -0.21875 to 0.21875
- w_down: bfloat16 [4, 2048, 768], P('expert', 'dp'), may hold values from -0.75 to 0.75
Outputs:
- output: bfloat16 [16, 2048, 768], P(('expert', 'dp'), 'context')
- grad_tokens: float32 [16, 2048, 768], P(('expert', 'dp'), 'context')
- grad_norm_one: float32 [768], P('dp')
- grad_w_query: float32 [768, 768], P('dp')
- grad_w_key: float32 [768, 768], P('dp')
- grad_w_value: float32 [768, 768], P('dp')
- grad_w_out: float32 [768, 768], P('dp')
- grad_norm_two: float32 [768], P('dp')
- grad_router: float32 [768, 8], P('dp')
- grad_w_res: float32 [8, 8], replicated
- grad_const_mix: float32 [768, 4], P('dp')
- grad_const_vec: float32 [768, 2], P('dp')
- grad_w_gate: float32 [4, 768, 2048], P('expert', 'dp')
- grad_w_up: float32 [4, 768, 2048], P('expert', 'dp')
- grad_w_down: float32 [4, 2048, 768], P('expert', 'dp')
Inputs may be any that keep to these rules, and one draw needn't show every extreme that they name: `segments`: segment numbers never fall along a sequence; the tokens with one number form one document. `routes`: each token names two different experts. In each block of 1024 consecutive tokens of a sequence the ranks are a permutation.
All inputs are finite; a program needn't handle non-finite values.
Results may differ from a plain program's by a relative error of at most 0.015.
Values may be sent and summed in bfloat16 or wider, within the bound.
A program may use at most 256 MiB of HBM per device.

v0:
```python
import jax
import jax.numpy as jnp
from jax import lax
from jax.sharding import PartitionSpec as P

D = 768
HEADS = 12
HEAD_DIM = 64
WIN = 1024
QB = 512
NZ = 4
TOK_DEV = 1024


EPS = 1e-05
MASKED = -1000000000.0
HIGH = lax.Precision.HIGHEST


def shifted(value, axis, steps):
    count = lax.axis_size(axis)
    first, last = (max(0, -steps), min(count, count - steps))
    return lax.ppermute(value, axis, [(source, source + steps) for source in range(first, last)])


def rms_norm(values, gain_vec):
    return values * lax.rsqrt(jnp.mean(values * values, axis=-1, keepdims=True) + EPS) * gain_vec


def rotary_tables(positions):
    half_dim = HEAD_DIM // 2
    frequency = 10000.0 ** (-jnp.arange(half_dim, dtype=jnp.float32) * 2.0 / HEAD_DIM)
    angles = positions.astype(jnp.float32)[:, None] * frequency[None, :]
    return (jnp.cos(angles)[:, None, :], jnp.sin(angles)[:, None, :])


def rotate(tensor, cos_table, sin_table):
    half_dim = HEAD_DIM // 2
    shaped = tensor.reshape(tensor.shape[0], HEADS, HEAD_DIM)
    first_half = shaped[..., :half_dim]
    second_half = shaped[..., half_dim:]
    turned = jnp.concatenate(
        [
            first_half * cos_table - second_half * sin_table,
            first_half * sin_table + second_half * cos_table,
        ],
        axis=-1,
    )
    return turned.reshape(tensor.shape)


def rotate_back(grad_rot, cos_table, sin_table):
    half_dim = HEAD_DIM // 2
    shaped = grad_rot.reshape(grad_rot.shape[0], HEADS, HEAD_DIM)
    first_half = shaped[..., :half_dim]
    second_half = shaped[..., half_dim:]
    turned = jnp.concatenate(
        [
            first_half * cos_table + second_half * sin_table,
            second_half * cos_table - first_half * sin_table,
        ],
        axis=-1,
    )
    return turned.reshape(grad_rot.shape)


def place_pairs(route_blk, rank_blk, experts, capacity):
    row_count = rank_blk.shape[0]
    token_ids = jnp.arange(row_count, dtype=jnp.int32)
    rank_order = jnp.zeros((row_count,), jnp.int32).at[rank_blk].set(token_ids)
    ordered = route_blk[rank_order].reshape(-1)
    onehot = (ordered[:, None] == jnp.arange(experts, dtype=jnp.int32)[None, :]).astype(jnp.int32)
    before = jnp.cumsum(onehot, axis=0) - onehot
    slot_ord = jnp.sum(before * onehot, axis=1).reshape(row_count, 2)
    slot_tok = slot_ord[rank_blk]
    kept_pair = (route_blk < experts) & (slot_tok < capacity)
    flat_index = jnp.where(kept_pair, route_blk * capacity + slot_tok, experts * capacity)
    pair_ids = jnp.arange(2 * row_count, dtype=jnp.int32)
    holder = (
        jnp.full((experts * capacity + 1,), 2 * row_count, jnp.int32)
        .at[flat_index.reshape(-1)]
        .set(pair_ids)
    )
    return (flat_index, holder[: experts * capacity])


def contract_last(left, right):
    return lax.dot_general(
        left, right, (((1,), (1,)), ((), ())), preferred_element_type=jnp.float32
    )


def contract_first(left, right):
    return lax.dot_general(
        left, right, (((0,), (0,)), ((), ())), preferred_element_type=jnp.float32
    )


def tile_total(pieces, blocks, group_count, tiles_per, group_width):
    shaped = pieces.reshape(blocks, group_count, tiles_per, QB, group_width)
    total = jnp.zeros((blocks + tiles_per - 1, group_count, QB, group_width), jnp.float32)
    for tile_pos in range(tiles_per):
        total = total + jnp.pad(
            shaped[:, :, tile_pos], ((tile_pos, tiles_per - 1 - tile_pos), (0, 0), (0, 0), (0, 0))
        )
    return total.transpose(0, 2, 1, 3).reshape(
        (blocks + tiles_per - 1) * QB, group_count * group_width
    )


def on_device(
    tokens,
    segments,
    routes,
    prev_logits,
    ranks,
    cotangent,
    norm_one,
    w_query,
    w_key,
    w_value,
    w_out,
    norm_two,
    router,
    w_res,
    const_mix,
    const_vec,
    w_gate,
    w_up,
    w_down,
):
    (
        gain_one,
        query_w,
        key_w,
        value_w,
        out_w,
        gain_two,
        router_w,
        mix_w,
        vec_w,
        gate_w,
        up_w,
        down_w,
    ) = (
        lax.all_gather(norm_one, "dp", axis=0, tiled=True),
        lax.all_gather(w_query, "dp", axis=0, tiled=True),
        lax.all_gather(w_key, "dp", axis=0, tiled=True),
        lax.all_gather(w_value, "dp", axis=0, tiled=True),
        lax.all_gather(w_out, "dp", axis=0, tiled=True),
        lax.all_gather(norm_two, "dp", axis=0, tiled=True),
        lax.all_gather(router, "dp", axis=0, tiled=True),
        lax.all_gather(const_mix, "dp", axis=0, tiled=True),
        lax.all_gather(const_vec, "dp", axis=0, tiled=True),
        lax.all_gather(w_gate, "dp", axis=1, tiled=True),
        lax.all_gather(w_up, "dp", axis=1, tiled=True),
        lax.all_gather(w_down, "dp", axis=1, tiled=True),
    )
    experts = lax.axis_size("expert")
    total_experts = experts + NZ
    capacity = (18 * TOK_DEV + 8 * total_experts - 1) // (8 * total_experts)
    scale_factor = HEAD_DIM ** (-0.5)
    head_group = 4
    group_count = HEADS // head_group
    group_width = head_group * HEAD_DIM
    blocks = TOK_DEV // QB
    span_len = WIN + QB
    tiles_per = span_len // QB
    offset = lax.axis_index("context") * TOK_DEV
    positions = offset + jnp.arange(TOK_DEV, dtype=jnp.int32)
    cos_table, sin_table = rotary_tables(positions)
    hidden_in = tokens[0].astype(jnp.float32)
    normed, norm_pull_one = jax.vjp(rms_norm, hidden_in, gain_one.astype(jnp.float32))
    normed_low = normed.astype(jnp.bfloat16)
    qkv_w = jnp.concatenate([query_w, key_w, value_w], axis=1)
    projected = jnp.dot(normed_low, qkv_w, preferred_element_type=jnp.float32)
    query_rot = rotate(projected[:, :D], cos_table, sin_table).astype(jnp.bfloat16)
    key_rot = rotate(projected[:, D : 2 * D], cos_table, sin_table).astype(jnp.bfloat16)
    value_low = projected[:, 2 * D :].astype(jnp.bfloat16)
    seg_local = segments[0]
    edge_keys, edge_values, edge_segs = shifted(
        (key_rot, value_low, seg_local.astype(jnp.bfloat16)), "context", 1
    )
    all_keys = jnp.concatenate([edge_keys, key_rot], axis=0)
    all_values = jnp.concatenate([edge_values, value_low], axis=0)
    all_segs = jnp.concatenate(
        [edge_segs.astype(jnp.float32), seg_local.astype(jnp.float32)], axis=0
    )
    all_pos = offset - WIN + jnp.arange(WIN + TOK_DEV, dtype=jnp.int32)

    def block_setup(block_item):
        block_id = block_item // group_count
        group_id = block_item % group_count
        row_start = block_id * QB
        column = group_id * group_width
        query_blk = lax.dynamic_slice(query_rot, (row_start, column), (QB, group_width)).reshape(
            QB, head_group, HEAD_DIM
        )
        key_blk = lax.dynamic_slice(all_keys, (row_start, column), (span_len, group_width)).reshape(
            span_len, head_group, HEAD_DIM
        )
        value_blk = lax.dynamic_slice(
            all_values, (row_start, column), (span_len, group_width)
        ).reshape(span_len, head_group, HEAD_DIM)
        query_pos = lax.dynamic_slice_in_dim(positions, row_start, QB, 0)
        key_pos = lax.dynamic_slice_in_dim(all_pos, row_start, span_len, 0)
        query_seg = lax.dynamic_slice_in_dim(all_segs, row_start + WIN, QB, 0)
        key_seg = lax.dynamic_slice_in_dim(all_segs, row_start, span_len, 0)
        distance = query_pos[:, None] - key_pos[None, :]
        allowed = (
            (key_pos[None, :] >= 0)
            & (distance >= 0)
            & (distance < WIN)
            & (query_seg[:, None] == key_seg[None, :])
        )
        raw_scores = jnp.einsum(
            "qhd,khd->hqk", query_blk, key_blk, preferred_element_type=jnp.float32
        )
        scores = jnp.where(allowed[None], raw_scores * scale_factor, MASKED)
        return (query_blk, key_blk, value_blk, scores, row_start, column)

    def attend(block_item):
        query_blk, key_blk, value_blk, scores, row_start, column = block_setup(block_item)
        row_peak = jnp.max(scores, axis=-1, keepdims=True)
        exp_scores = jnp.exp(scores - row_peak)
        row_total = jnp.sum(exp_scores, axis=-1, keepdims=True)
        weights = (exp_scores / row_total).astype(jnp.bfloat16)
        mixed_rows = jnp.einsum(
            "hqk,khd->qhd", weights, value_blk, preferred_element_type=jnp.float32
        ).reshape(QB, group_width)
        return (mixed_rows, (row_peak + jnp.log(row_total))[..., 0])

    block_items = jnp.arange(blocks * group_count, dtype=jnp.int32)
    pieces, log_totals = lax.map(attend, block_items)
    attended = (
        pieces.reshape(blocks, group_count, QB, group_width)
        .transpose(0, 2, 1, 3)
        .reshape(TOK_DEV, D)
    )
    attn_low = attended.astype(jnp.bfloat16)
    residual = hidden_in + jnp.dot(attn_low, out_w, preferred_element_type=jnp.float32)
    normed_two, norm_pull_two = jax.vjp(rms_norm, residual, gain_two.astype(jnp.float32))
    low_two = normed_two.astype(jnp.bfloat16)
    route_w = jnp.concatenate([router_w, mix_w], axis=1)
    route_out = jnp.dot(low_two, route_w, preferred_element_type=jnp.float32)
    route_ids = routes[0]
    prev_local = prev_logits[0]
    logits = route_out[:, :total_experts] + jnp.dot(
        prev_local, w_res.astype(jnp.float32), precision=HIGH
    )
    mix_logit = route_out[:, total_experts:].reshape(TOK_DEV, 2, 2)
    router_probs = jax.nn.softmax(logits, axis=-1)
    choose_hot = (
        route_ids[:, :, None] == jnp.arange(total_experts, dtype=jnp.int32)[None, None, :]
    ).astype(jnp.float32)
    gate_values = jnp.sum(choose_hot * router_probs[:, None, :], axis=-1)
    flat_index, holder = place_pairs(route_ids, ranks[0, 0], experts, capacity)
    token_src = jnp.where(holder < 2 * TOK_DEV, holder // 2, TOK_DEV)
    padded_low = jnp.concatenate([low_two, jnp.zeros((1, D), jnp.bfloat16)], axis=0)
    outgoing = padded_low[token_src].reshape(experts, capacity, D)
    incoming = lax.all_to_all(outgoing, "expert", split_axis=0, concat_axis=0, tiled=True).reshape(
        experts * capacity, D
    )
    gate_pre = jnp.dot(incoming, gate_w[0], preferred_element_type=jnp.float32)
    up_pre = jnp.dot(incoming, up_w[0], preferred_element_type=jnp.float32)
    sigmoid_gate = jax.nn.sigmoid(gate_pre)
    swish_gate = gate_pre * sigmoid_gate
    hidden_low = (swish_gate * up_pre).astype(jnp.bfloat16)
    expert_rows = jnp.dot(hidden_low, down_w[0], preferred_element_type=jnp.float32).astype(
        jnp.bfloat16
    )
    returned = lax.all_to_all(
        expert_rows.reshape(experts, capacity, D), "expert", split_axis=0, concat_axis=0, tiled=True
    ).reshape(experts * capacity, D)
    padded_back = jnp.concatenate([returned, jnp.zeros((1, D), jnp.bfloat16)], axis=0)
    ffn_out = padded_back[flat_index].astype(jnp.float32)
    mix_prob = jax.nn.softmax(mix_logit, axis=-1)
    const_vecs = vec_w.astype(jnp.float32)
    const_out = (
        mix_prob[:, :, 0:1] * normed_two[:, None, :]
        + mix_prob[:, :, 1:2] * const_vecs.T[None, :, :]
    )
    chosen = route_ids[:, :, None]
    expert_out = (
        jnp.where(chosen < experts, ffn_out, 0.0)
        + jnp.where(chosen == experts + 1, normed_two[:, None, :], 0.0)
        + jnp.where(chosen == experts + 2, const_out[:, 0:1, :], 0.0)
        + jnp.where(chosen == experts + 3, const_out[:, 1:2, :], 0.0)
    )
    moe_out = jnp.sum(gate_values[:, :, None] * expert_out, axis=1)
    output = (residual + moe_out).astype(jnp.bfloat16)[None]
    grad_out = cotangent[0].astype(jnp.float32)
    grad_gates = jnp.sum(grad_out[:, None, :] * expert_out, axis=-1)
    pair_grad = (
        (gate_values[:, :, None] * grad_out[:, None, :])
        .astype(jnp.bfloat16)
        .reshape(2 * TOK_DEV, D)
    )
    padded_pairs = jnp.concatenate([pair_grad, jnp.zeros((1, D), jnp.bfloat16)], axis=0)
    grad_send = padded_pairs[holder].reshape(experts, capacity, D)
    grad_rows = lax.all_to_all(
        grad_send, "expert", split_axis=0, concat_axis=0, tiled=True
    ).reshape(experts * capacity, D)
    grad_hidden = contract_last(grad_rows, down_w[0])
    grad_down_w = contract_first(hidden_low, grad_rows)
    grad_gate = (
        grad_hidden * up_pre * sigmoid_gate * (1.0 + gate_pre * (1.0 - sigmoid_gate))
    ).astype(jnp.bfloat16)
    grad_up = (grad_hidden * swish_gate).astype(jnp.bfloat16)
    grad_rows_in = (contract_last(grad_gate, gate_w[0]) + contract_last(grad_up, up_w[0])).astype(
        jnp.bfloat16
    )
    grad_gate_w = contract_first(incoming, grad_gate)
    grad_up_w = contract_first(incoming, grad_up)
    grad_back = lax.all_to_all(
        grad_rows_in.reshape(experts, capacity, D),
        "expert",
        split_axis=0,
        concat_axis=0,
        tiled=True,
    ).reshape(experts * capacity, D)
    padded_grad = jnp.concatenate([grad_back, jnp.zeros((1, D), jnp.bfloat16)], axis=0)
    grad_from_ffn = jnp.sum(padded_grad[flat_index].astype(jnp.float32), axis=1)
    copy_weight = jnp.sum(jnp.where(route_ids == experts + 1, gate_values, 0.0), axis=1)
    const_weight = jnp.stack(
        [
            jnp.sum(jnp.where(route_ids == experts + 2, gate_values, 0.0), axis=1),
            jnp.sum(jnp.where(route_ids == experts + 3, gate_values, 0.0), axis=1),
        ],
        axis=1,
    )
    dot_normed = jnp.sum(grad_out * normed_two, axis=-1)
    dot_vec = jnp.sum(grad_out[:, None, :] * const_vecs.T[None, :, :], axis=-1)
    grad_vec = jnp.sum(
        grad_out[:, None, :] * (const_weight * mix_prob[:, :, 1])[:, :, None], axis=0
    ).T
    grad_mix_prob = const_weight[:, :, None] * jnp.stack(
        [jnp.broadcast_to(dot_normed[:, None], (TOK_DEV, 2)), dot_vec], axis=-1
    )
    grad_mix_logit = mix_prob * (
        grad_mix_prob - jnp.sum(mix_prob * grad_mix_prob, axis=-1, keepdims=True)
    )
    grad_probs = jnp.sum(choose_hot * grad_gates[:, :, None], axis=1)
    grad_logits = router_probs * (
        grad_probs - jnp.sum(router_probs * grad_probs, axis=-1, keepdims=True)
    )
    res_part = lax.dot_general(
        prev_local,
        grad_logits,
        (((0,), (0,)), ((), ())),
        precision=HIGH,
        preferred_element_type=jnp.float32,
    )
    grad_res_total = lax.psum(res_part, ("expert", "context", "dp"))
    grad_route = jnp.concatenate([grad_logits, grad_mix_logit.reshape(TOK_DEV, 4)], axis=1).astype(
        jnp.bfloat16
    )
    grad_route_w = contract_first(low_two, grad_route)
    grad_normed_two = (
        copy_weight[:, None] * grad_out
        + jnp.sum(const_weight[:, :, None] * mix_prob[:, :, 0:1], axis=1) * grad_out
        + contract_last(grad_route, route_w)
        + grad_from_ffn
    )
    grad_resid_norm, grad_gain_two = norm_pull_two(grad_normed_two)
    grad_resid = grad_out + grad_resid_norm
    grad_attn_low = grad_resid.astype(jnp.bfloat16)
    grad_out_w = contract_first(attn_low, grad_attn_low)
    grad_attended = contract_last(grad_attn_low, out_w).astype(jnp.bfloat16)

    def attend_back(block_item):
        query_blk, key_blk, value_blk, scores, row_start, column = block_setup(block_item)
        probs_blk = jnp.exp(scores - log_totals[block_item][..., None])
        weights = probs_blk.astype(jnp.bfloat16)
        grad_blk = lax.dynamic_slice(grad_attended, (row_start, column), (QB, group_width)).reshape(
            QB, head_group, HEAD_DIM
        )
        grad_weights = jnp.einsum(
            "qhd,khd->hqk", grad_blk, value_blk, preferred_element_type=jnp.float32
        )
        inner = jnp.sum(probs_blk * grad_weights, axis=-1, keepdims=True)
        grad_scores = (probs_blk * (grad_weights - inner) * scale_factor).astype(jnp.bfloat16)
        grad_query_blk = jnp.einsum(
            "hqk,khd->qhd", grad_scores, key_blk, preferred_element_type=jnp.float32
        ).reshape(QB, group_width)
        grad_key_blk = jnp.einsum(
            "hqk,qhd->khd", grad_scores, query_blk, preferred_element_type=jnp.float32
        ).reshape(span_len, group_width)
        grad_value_blk = jnp.einsum(
            "hqk,qhd->khd", weights, grad_blk, preferred_element_type=jnp.float32
        ).reshape(span_len, group_width)
        return (grad_query_blk, grad_key_blk, grad_value_blk)

    grad_query_pieces, key_pieces, value_pieces = lax.map(attend_back, block_items)
    key_acc = tile_total(key_pieces, blocks, group_count, tiles_per, group_width)
    value_acc = tile_total(value_pieces, blocks, group_count, tiles_per, group_width)
    grad_query_rot = (
        grad_query_pieces.reshape(blocks, group_count, QB, group_width)
        .transpose(0, 2, 1, 3)
        .reshape(TOK_DEV, D)
    )
    returned_keys, returned_values = (
        shifted(key_acc[:WIN].astype(jnp.bfloat16), "context", -1).astype(jnp.float32),
        shifted(value_acc[:WIN].astype(jnp.bfloat16), "context", -1).astype(jnp.float32),
    )
    edge_pad = jnp.zeros((TOK_DEV - WIN, D), jnp.float32)
    grad_key_rot = key_acc[WIN:] + jnp.concatenate([edge_pad, returned_keys], axis=0)
    grad_value = value_acc[WIN:] + jnp.concatenate([edge_pad, returned_values], axis=0)
    grad_qkv = jnp.concatenate(
        [
            rotate_back(grad_query_rot, cos_table, sin_table),
            rotate_back(grad_key_rot, cos_table, sin_table),
            grad_value,
        ],
        axis=1,
    ).astype(jnp.bfloat16)
    grad_normed_one = contract_last(grad_qkv, qkv_w)
    grad_qkv_w = contract_first(normed_low, grad_qkv)
    grad_in_norm, grad_gain_one = norm_pull_one(grad_normed_one)
    grad_tokens = (grad_resid + grad_in_norm)[None]
    grad_query_w = grad_qkv_w[:, :D]
    grad_key_w = grad_qkv_w[:, D : 2 * D]
    grad_value_w = grad_qkv_w[:, 2 * D :]
    grad_router_w = grad_route_w[:, :total_experts]
    grad_mix_w = grad_route_w[:, total_experts:]
    (
        sum_gain_one,
        sum_query,
        sum_key,
        sum_value,
        sum_out,
        sum_gain_two,
        sum_router,
        sum_mix,
        sum_vec,
    ) = lax.psum(
        (
            grad_gain_one,
            grad_query_w,
            grad_key_w,
            grad_value_w,
            grad_out_w,
            grad_gain_two,
            grad_router_w,
            grad_mix_w,
            grad_vec,
        ),
        ("expert", "context"),
    )
    (
        share_gain_one,
        share_query,
        share_key,
        share_value,
        share_out,
        share_gain_two,
        share_router,
        share_mix,
        share_vec,
        share_gate,
        share_up,
        share_down,
    ) = (
        lax.psum_scatter(sum_gain_one, "dp", scatter_dimension=0, tiled=True),
        lax.psum_scatter(sum_query, "dp", scatter_dimension=0, tiled=True),
        lax.psum_scatter(sum_key, "dp", scatter_dimension=0, tiled=True),
        lax.psum_scatter(sum_value, "dp", scatter_dimension=0, tiled=True),
        lax.psum_scatter(sum_out, "dp", scatter_dimension=0, tiled=True),
        lax.psum_scatter(sum_gain_two, "dp", scatter_dimension=0, tiled=True),
        lax.psum_scatter(sum_router, "dp", scatter_dimension=0, tiled=True),
        lax.psum_scatter(sum_mix, "dp", scatter_dimension=0, tiled=True),
        lax.psum_scatter(sum_vec, "dp", scatter_dimension=0, tiled=True),
        lax.psum_scatter(grad_gate_w[None], "dp", scatter_dimension=1, tiled=True),
        lax.psum_scatter(grad_up_w[None], "dp", scatter_dimension=1, tiled=True),
        lax.psum_scatter(grad_down_w[None], "dp", scatter_dimension=1, tiled=True),
    )
    total_gate, total_up, total_down = lax.psum((share_gate, share_up, share_down), "context")
    return (
        output,
        grad_tokens,
        share_gain_one,
        share_query,
        share_key,
        share_value,
        share_out,
        share_gain_two,
        share_router,
        grad_res_total,
        share_mix,
        share_vec,
        total_gate,
        total_up,
        total_down,
    )


def solution(mesh):
    in_specs = (
        P(("expert", "dp"), "context", None),
        P(("expert", "dp"), "context"),
        P(("expert", "dp"), "context", None),
        P(("expert", "dp"), "context", None),
        P(("expert", "dp"), "context", None),
        P(("expert", "dp"), "context", None),
        P("dp"),
        P("dp", None),
        P("dp", None),
        P("dp", None),
        P("dp", None),
        P("dp"),
        P("dp", None),
        P(),
        P("dp", None),
        P("dp", None),
        P("expert", "dp", None),
        P("expert", "dp", None),
        P("expert", "dp", None),
    )
    out_specs = (
        P(("expert", "dp"), "context", None),
        P(("expert", "dp"), "context", None),
        P("dp"),
        P("dp", None),
        P("dp", None),
        P("dp", None),
        P("dp", None),
        P("dp"),
        P("dp", None),
        P(),
        P("dp", None),
        P("dp", None),
        P("expert", "dp", None),
        P("expert", "dp", None),
        P("expert", "dp", None),
    )
    return jax.shard_map(
        on_device, mesh=mesh, in_specs=in_specs, out_specs=out_specs, check_vma=False
    )
```

profile of v0, /device:TPU:19, one launch (start us, length us, event | category | flops | bytes accessed | tf_op | source)
XLA Modules:
  0.0 1712.1 jit_solution(4708387665391693804)
XLA Ops:
  54.2 10.1 all-gather
  79.7 23.4 %all-gather.15.cloned.1.call-done = bf16[768,768]{1,0:T(8,128)(2,1)} async-done(((bf16[192,768]{1,0:T(8,128)(2,1)}), bf16[768,768]{1,0:T(8,128)(2,1)}) %all-gather.15.cloned.1.call-update) | async-done | bytes 1179664 | tf_op jit(solution)/shard_map/all_gather | solution.py:149
  167.1 117.4 %while.32 = (s32[]{:T(128)}, bf16[6,512,256]{1,2,0:T(8,128)(2,1)}, f32[6,4,512]{2,1,0:T(4,128)}, s32[6]{0:T(128)S(1)}, bf16[2048,768]{0,1:T(8,128)(2,1)}, /*inde...) while((s32[]{:T(128)}, bf16[6,512,256]{1,2,0:T(8,128)(2,1)}, ...), condition=%wide.region_4.5_spmd.clone, body=%wide.region_1.4_spmd.sunk.clone | while | flops 848559616 | bytes 47304120 | solution.py:234
  360.9 18.2 %multiply_convert_fusion.1 = (bf16[1152,2048]{1,0:T(8,128)(2,1)}, bf16[1152,2048]{1,0:T(8,128)(2,1)}, bf16[1152,2048]{1,0:T(8,128)(2,1)}) fusion(f32[1152,2048]{1,0:T(8,128)} %fusion.48, f32[1152,2048]{1,0:T(8,128)} %fusion.44, bf16[1152,768]{1,0:T(8,128)(2,1)S(1)} %bitcast.396, bf16[1,2048,768]{2,1,0:T(8,128)(2,1)} %all-gather.23.cloned.1.call-done), kind=kOutput, calls=%fused_computation.49 | convolution fusion | flops 3659268096 | bytes 37945344 | tf_op jit(solution)/shard_map/dot_general | solution.py:88
  415.9 12.0 fusion.96
  438.4 12.0 gather_fusion.5
  467.8 34.0 %multiply_reduce_fusion.3 = (f32[1024,2]{1,0:T(8,128)}, f32[1024,768]{1,0:T(8,128)}, f32[2,768]{1,0:T(2,128)}, f32[1024,2]{1,0:T(8,128)S(1)}) fusion(f32[1024,768]{1,0:T(8,128)} %bitcast_convert_fusion, f32[1024,2]{1,0:T(8,128)} %copy-done.26, f32[1024,2]{1,0:T(8,128)} %get-tuple-element.774, f32[2,768]{1,0:T(2,128)S(1)} %bitcast.407, ...), kind=kLoop, calls=%fused_computation.64 | loop fusion | flops 22800896 | bytes 22073344 | tf_op jit(solution)/shard_map/reduce_sum | solution.py:293
  511.3 12.1 reduce_sum.264
  539.1 433.5 %while.33 = (s32[]{:T(128)}, f32[6,512,256]{1,2,0:T(8,128)}, f32[6,1536,256]{2,1,0:T(8,128)}, f32[6,1536,256]{2,1,0:T(8,128)}, s32[6]{0:T(128)S(1)}, /*index=5*/...) while((s32[]{:T(128)}, f32[6,512,256]{1,2,0:T(8,128)}, ...), condition=%wide.region_31.32_spmd.clone, body=%wide.region_29.31_spmd.sunk.clone | while | flops 2062819840 | bytes 173878896 | solution.py:394
  568.5 19.3 %fusion.197 = f32[4,64,512]{2,1,0:T(8,128)} fusion(bf16[1536,4,64]{0,2,1:T(8,128)(2,1)S(1)} %bitcast.371, f32[4,512,1536]{2,1,0:T(8,128)} %copy-done.1, f32[4,512,1536]{2,1,0:T(8,128)} %fusion.196), kind=kOutput, calls=%fused_computation.30.clone.1.clone | convolution fusion | flops 418385408 | bytes 26476544 | tf_op jit(solution)/shard_map/while/body/eval_jaxpr/hqk,khd->qhd/dot_general | solution.py:383
  587.7 18.1 %fusion.199 = f32[4,64,1536]{2,1,0:T(8,128)} fusion(bf16[512,4,64]{0,2,1:T(8,128)(2,1)S(1)} %bitcast.388, f32[4,512,1536]{2,1,0:T(8,128)} %copy-done.1, f32[4,512,1536]{2,1,0:T(8,128)} %fusion.196), kind=kOutput, calls=%fused_computation.29.clone.1.clone | convolution fusion | flops 418385408 | bytes 27000832 | tf_op jit(solution)/shard_map/while/body/eval_jaxpr/hqk,qhd->khd/dot_general | solution.py:386
  640.6 19.3 %fusion.197 = f32[4,64,512]{2,1,0:T(8,128)} fusion(bf16[1536,4,64]{0,2,1:T(8,128)(2,1)S(1)} %bitcast.371, f32[4,512,1536]{2,1,0:T(8,128)} %copy-done.1, f32[4,512,1536]{2,1,0:T(8,128)} %fusion.196), kind=kOutput, calls=%fused_computation.30.clone.1.clone | convolution fusion | flops 418385408 | bytes 26476544 | tf_op jit(solution)/shard_map/while/body/eval_jaxpr/hqk,khd->qhd/dot_general | solution.py:383
  659.9 18.1 %fusion.199 = f32[4,64,1536]{2,1,0:T(8,128)} fusion(bf16[512,4,64]{0,2,1:T(8,128)(2,1)S(1)} %bitcast.388, f32[4,512,1536]{2,1,0:T(8,128)} %copy-done.1, f32[4,512,1536]{2,1,0:T(8,128)} %fusion.196), kind=kOutput, calls=%fused_computation.29.clone.1.clone | convolution fusion | flops 418385408 | bytes 27000832 | tf_op jit(solution)/shard_map/while/body/eval_jaxpr/hqk,qhd->khd/dot_general | solution.py:386
  712.7 19.3 %fusion.197 = f32[4,64,512]{2,1,0:T(8,128)} fusion(bf16[1536,4,64]{0,2,1:T(8,128)(2,1)S(1)} %bitcast.371, f32[4,512,1536]{2,1,0:T(8,128)} %copy-done.1, f32[4,512,1536]{2,1,0:T(8,128)} %fusion.196), kind=kOutput, calls=%fused_computation.30.clone.1.clone | convolution fusion | flops 418385408 | bytes 26476544 | tf_op jit(solution)/shard_map/while/body/eval_jaxpr/hqk,khd->qhd/dot_general | solution.py:383
  732.0 18.1 %fusion.199 = f32[4,64,1536]{2,1,0:T(8,128)} fusion(bf16[512,4,64]{0,2,1:T(8,128)(2,1)S(1)} %bitcast.388, f32[4,512,1536]{2,1,0:T(8,128)} %copy-done.1, f32[4,512,1536]{2,1,0:T(8,128)} %fusion.196), kind=kOutput, calls=%fused_computation.29.clone.1.clone | convolution fusion | flops 418385408 | bytes 27000832 | tf_op jit(solution)/shard_map/while/body/eval_jaxpr/hqk,qhd->khd/dot_general | solution.py:386
  785.0 19.3 %fusion.197 = f32[4,64,512]{2,1,0:T(8,128)} fusion(bf16[1536,4,64]{0,2,1:T(8,128)(2,1)S(1)} %bitcast.371, f32[4,512,1536]{2,1,0:T(8,128)} %copy-done.1, f32[4,512,1536]{2,1,0:T(8,128)} %fusion.196), kind=kOutput, calls=%fused_computation.30.clone.1.clone | convolution fusion | flops 418385408 | bytes 26476544 | tf_op jit(solution)/shard_map/while/body/eval_jaxpr/hqk,khd->qhd/dot_general | solution.py:383
  804.2 18.1 %fusion.199 = f32[4,64,1536]{2,1,0:T(8,128)} fusion(bf16[512,4,64]{0,2,1:T(8,128)(2,1)S(1)} %bitcast.388, f32[4,512,1536]{2,1,0:T(8,128)} %copy-done.1, f32[4,512,1536]{2,1,0:T(8,128)} %fusion.196), kind=kOutput, calls=%fused_computation.29.clone.1.clone | convolution fusion | flops 418385408 | bytes 27000832 | tf_op jit(solution)/shard_map/while/body/eval_jaxpr/hqk,qhd->khd/dot_general | solution.py:386
  857.1 19.3 %fusion.197 = f32[4,64,512]{2,1,0:T(8,128)} fusion(bf16[1536,4,64]{0,2,1:T(8,128)(2,1)S(1)} %bitcast.371, f32[4,512,1536]{2,1,0:T(8,128)} %copy-done.1, f32[4,512,1536]{2,1,0:T(8,128)} %fusion.196), kind=kOutput, calls=%fused_computation.30.clone.1.clone | convolution fusion | flops 418385408 | bytes 26476544 | tf_op jit(solution)/shard_map/while/body/eval_jaxpr/hqk,khd->qhd/dot_general | solution.py:383
  876.3 18.1 %fusion.199 = f32[4,64,1536]{2,1,0:T(8,128)} fusion(bf16[512,4,64]{0,2,1:T(8,128)(2,1)S(1)} %bitcast.388, f32[4,512,1536]{2,1,0:T(8,128)} %copy-done.1, f32[4,512,1536]{2,1,0:T(8,128)} %fusion.196), kind=kOutput, calls=%fused_computation.29.clone.1.clone | convolution fusion | flops 418385408 | bytes 27000832 | tf_op jit(solution)/shard_map/while/body/eval_jaxpr/hqk,qhd->khd/dot_general | solution.py:386
  929.2 19.3 %fusion.197 = f32[4,64,512]{2,1,0:T(8,128)} fusion(bf16[1536,4,64]{0,2,1:T(8,128)(2,1)S(1)} %bitcast.371, f32[4,512,1536]{2,1,0:T(8,128)} %copy-done.1, f32[4,512,1536]{2,1,0:T(8,128)} %fusion.196), kind=kOutput, calls=%fused_computation.30.clone.1.clone | convolution fusion | flops 418385408 | bytes 26476544 | tf_op jit(solution)/shard_map/while/body/eval_jaxpr/hqk,khd->qhd/dot_general | solution.py:383
  948.5 18.1 %fusion.199 = f32[4,64,1536]{2,1,0:T(8,128)} fusion(bf16[512,4,64]{0,2,1:T(8,128)(2,1)S(1)} %bitcast.388, f32[4,512,1536]{2,1,0:T(8,128)} %copy-done.1, f32[4,512,1536]{2,1,0:T(8,128)} %fusion.196), kind=kOutput, calls=%fused_computation.29.clone.1.clone | convolution fusion | flops 418385408 | bytes 27000832 | tf_op jit(solution)/shard_map/while/body/eval_jaxpr/hqk,qhd->khd/dot_general | solution.py:386
  1079.7 10.9 reduce-scatter.27.cloned.1.call-done
  1090.6 49.7 %reduce-scatter.25.cloned.1.call-done = f32[192,768]{1,0:T(8,128)} async-done(((f32[768,768]{1,0:T(8,128)}), f32[192,768]{1,0:T(8,128)}) %reduce-scatter.25.cloned.1.call-update) | async-done | bytes 589840 | tf_op jit(solution)/shard_map/reduce_scatter | solution.py:466
  1140.3 49.9 %reduce-scatter.23.cloned.1.call-done = f32[192,768]{1,0:T(8,128)} async-done(((f32[768,768]{1,0:T(8,128)}), f32[192,768]{1,0:T(8,128)}) %reduce-scatter.23.cloned.1.call-update) | async-done | bytes 589840 | tf_op jit(solution)/shard_map/reduce_scatter | solution.py:465
  1190.3 113.4 %reduce-scatter.17.cloned.1.call-done = f32[1,192,2048]{2,1,0:T(8,128)} async-done(((f32[1,768,2048]{2,1,0:T(8,128)}), f32[1,192,2048]{2,1,0:T(8,128)}) %reduce-scatter.17.cloned.1.call-update) | async-done | bytes 1572880 | tf_op jit(solution)/shard_map/reduce_scatter | solution.py:473
  1303.7 113.6 %reduce-scatter.19.cloned.1.call-done = f32[1,192,2048]{2,1,0:T(8,128)} async-done(((f32[1,768,2048]{2,1,0:T(8,128)}), f32[1,192,2048]{2,1,0:T(8,128)}) %reduce-scatter.19.cloned.1.call-update) | async-done | bytes 1572880 | tf_op jit(solution)/shard_map/reduce_scatter | solution.py:474
  1417.3 113.5 %reduce-scatter.21.cloned.1.call-done = f32[1,512,768]{2,1,0:T(8,128)} async-done(((f32[1,2048,768]{2,1,0:T(8,128)}), f32[1,512,768]{2,1,0:T(8,128)}) %reduce-scatter.21.cloned.1.call-update) | async-done | bytes 1572880 | tf_op jit(solution)/shard_map/reduce_scatter | solution.py:475
  1531.6 38.5 %psum.98 = f32[8,8]{0,1:T(8,128)S(1)} all-reduce(f32[8,8]{0,1:T(8,128)S(1)} %convolution_bitcast_fusion.3), channel_id=1, replica_groups=mesh['expert'=4,'context'=2,'dp'=4] {'expert','context','dp'}, use_global_device_ids=true, to_apply=%region_49.50 | all-reduce | flops 64 | bytes 512 | tf_op jit(solution)/shard_map/psum | solution.py:354
  1574.0 20.6 %reduce-scatter.31.cloned.1.call-done = f32[192,8]{1,0:T(8,128)} async-done(((f32[768,8]{1,0:T(8,128)}), f32[192,8]{1,0:T(8,128)}) %reduce-scatter.31.cloned.1.call-update) | async-done | bytes 6160
  1611.3 24.3 %all-reduce.14 = (f32[192]{0:T(256)}, f32[192]{0:T(256)}, f32[192,8]{0,1:T(8,128)}, f32[192,4]{0,1:T(4,128)}, f32[192,2]{0,1:T(2,128)}) all-reduce(f32[192]{0:T(256)S(1)} %dynamic-slice.3, f32[192]{0:T(256)S(1)} %dynamic-slice.5, f32[192,8]{0,1:T(8,128)S(1)} %copy.340, ...), channel_id=1, replica_groups=mesh['expert'=4,'context'=2,'dp'=4] {'expert','context'}, use_global_device_ids=true, to_apply=%region_34.35 | all-reduce | flops 3072 | bytes 24576 | tf_op jit(solution)/shard_map/psum | solution.py:436
  1640.5 21.6 %all-reduce.22.cloned.1.call-done = (f32[192,768]{1,0:T(8,128)}, f32[192,768]{1,0:T(8,128)}, f32[192,768]{1,0:T(8,128)}, f32[192,768]{1,0:T(8,128)}) async-done(((f32[192,768]{1,0:T(8,128)}, f32[192,768]{1,0:T(8,128)}, f32[192,768]{1,0:T(8,128)}, f32[192,768]{1,0:T(8,128)}), (f32[192,768]{1,0:T(8,128)}, f32[192,768]{1,0:T(8,128)}, f32[192,768]{1,0:T(8,128)}, ...) | async-done | bytes 2359312 | tf_op jit(solution)/shard_map/psum | solution.py:436
  1662.1 33.0 %all-reduce.24.cloned.1.call-done = (f32[1,192,2048]{2,1,0:T(8,128)}, f32[1,192,2048]{2,1,0:T(8,128)}, f32[1,512,768]{2,1,0:T(8,128)}) async-done(((f32[1,192,2048]{2,1,0:T(8,128)}, f32[1,192,2048]{2,1,0:T(8,128)}, f32[1,512,768]{2,1,0:T(8,128)}), (f32[1,192,2048]{2,1,0:T(8,128)}, f32[1,192,2048]{2,1,0:T(8,128)}, f32[1,512,768]{2,1,0:T(8,128)})) %all-reduce.24.cloned.1.call-update) | async-done | bytes 4718608 | tf_op jit(solution)/shard_map/psum | solution.py:477
  (699 shorter events, 723.0 us)
Async XLA Ops:
  7.2 290.4 %copy-start = (f32[1,1024,8]{1,2,0:T(8,128)S(1)}, f32[1,1024,8]{1,2,0:T(8,128)}, u32[]{:S(2)}) copy-start(f32[1,1024,8]{1,2,0:T(8,128)} %param.26) | copy-start | bytes 98308
  7.2 67.7 %all-gather.11.cloned.1.call-start = ((), (), s32[]{:S(2)}) async-start(), calls=%async_computation.14 | async-start | bytes 1474560 | tf_op jit(solution)/shard_map/all_gather | solution.py:147
  7.9 69.4 %all-gather.13.cloned.1.call-start = ((), (), s32[]{:S(2)}) async-start(), calls=%async_computation.15 | async-start | bytes 1474560 | tf_op jit(solution)/shard_map/all_gather | solution.py:148
  8.7 94.5 %all-gather.15.cloned.1.call-start = ((), (), s32[]{:S(2)}) async-start(), calls=%async_computation.16 | async-start | bytes 1474560 | tf_op jit(solution)/shard_map/all_gather | solution.py:149
  9.4 279.6 %all-gather.17.cloned.1.call-start = ((), (), s32[]{:S(2)}) async-start(), calls=%async_computation.17 | async-start | bytes 1474560 | tf_op jit(solution)/shard_map/all_gather | solution.py:150
  10.0 331.0 %all-gather.21.cloned.1.call-start = ((), (), s32[]{:S(2)}) async-start(), calls=%async_computation.19 | async-start | bytes 3932160 | tf_op jit(solution)/shard_map/all_gather | solution.py:156
  10.6 340.3 %all-gather.19.cloned.1.call-start = ((), (), s32[]{:S(2)}) async-start(), calls=%async_computation.18 | async-start | bytes 3932160 | tf_op jit(solution)/shard_map/all_gather | solution.py:155
  11.2 349.7 %all-gather.23.cloned.1.call-start = ((), (), s32[]{:S(2)}) async-start(), calls=%async_computation.20 | async-start | bytes 3932160 | tf_op jit(solution)/shard_map/all_gather | solution.py:157
  11.9 140.2 %collective-permute-start.1 = (bf16[1024]{0:T(1024)(128)(2,1)S(1)}, bf16[1024]{0:T(1024)(128)(2,1)S(1)}, u32[]{:S(2)}, u32[]{:S(2)}) collective-permute-start(bf16[1024]{0:T(1024)(128)(2,1)S(1)} %convert_reduce_fusion), channel_id=1, source_target_pairs={{0,4},{1,5},{2,6},{3,7},{8,12},{9,13},{10,14},{11,15},{16,20},{17,... | collective-permute-start | bytes 6152 | tf_op jit(solution)/shard_map/ppermute | solution.py:23
  119.5 35.1 %collective-permute-start = (bf16[1024,768]{1,0:T(8,128)(2,1)}, bf16[1024,768]{1,0:T(8,128)(2,1)}, u32[]{:S(2)}, u32[]{:S(2)}) collective-permute-start(bf16[1024,768]{1,0:T(8,128)(2,1)} %slice.237), channel_id=1, source_target_pairs={{0,4},{1,5},{2,6},{3,7},{8,12},{9,13},{10,14},{11,15},{16,20},{17,... | collective-permute-start | bytes 4718600 | tf_op jit(solution)/shard_map/ppermute | solution.py:23
  130.5 32.7 %collective-permute-start.2 = (bf16[1024,768]{0,1:T(8,128)(2,1)}, bf16[1024,768]{0,1:T(8,128)(2,1)}, u32[]{:S(2)}, u32[]{:S(2)}) collective-permute-start(bf16[1024,768]{0,1:T(8,128)(2,1)} %bitcast.28), channel_id=1, source_target_pairs={{0,4},{1,5},{2,6},{3,7},{8,12},{9,13},{10,14},{11,15},{16,20},{17,... | collective-permute-start | bytes 4718600 | tf_op jit(solution)/shard_map/ppermute | solution.py:23
  305.0 32.2 %all-to-all-start = ((bf16[4,288,768]{2,1,0:T(8,128)(2,1)}), bf16[4,288,768]{2,1,0:T(8,128)(2,1)}, u32[]{:S(2)}, u32[]{:S(2)}) async-start(bf16[4,288,768]{2,1,0:T(8,128)(2,1)} %bitcast.384), calls=%async_computation | async-start | bytes 3538944 | tf_op jit(solution)/shard_map/all_to_all | solution.py:261
  337.2 23.7 %all-to-all-start.2 = ((bf16[4,288,768]{2,1,0:T(8,128)(2,1)}), bf16[4,288,768]{2,1,0:T(8,128)(2,1)S(1)}, u32[]{:S(2)}, u32[]{:S(2)}) async-start(bf16[4,288,768]{2,1,0:T(8,128)(2,1)} %bitcast.60), calls=%async_computation.2 | async-start | bytes 3538944 | tf_op jit(solution)/shard_map/all_to_all | solution.py:301
  386.5 21.0 %all-to-all-start.1 = ((bf16[4,288,768]{2,1,0:T(8,128)(2,1)}), bf16[4,288,768]{2,1,0:T(8,128)(2,1)S(1)}, u32[]{:S(2)}, u32[]{:S(2)}) async-start(bf16[4,288,768]{2,1,0:T(8,128)(2,1)} %bitcast.399), calls=%async_computation.1 | async-start | bytes 3538944 | tf_op jit(solution)/shard_map/all_to_all | solution.py:272
  407.5 28.0 %all-to-all-start.3 = ((bf16[4,288,768]{2,1,0:T(8,128)(2,1)}), bf16[4,288,768]{2,1,0:T(8,128)(2,1)}, u32[]{:S(2)}, u32[]{:S(2)}) async-start(bf16[4,288,768]{2,1,0:T(8,128)(2,1)} %bitcast.398), calls=%async_computation.3 | async-start | bytes 3538944 | tf_op jit(solution)/shard_map/all_to_all | solution.py:315
  415.9 663.9 %reduce-scatter.29.cloned.1.call-start = ((), (), s32[]{:S(2)}) async-start(), calls=%async_computation.27 | async-start | bytes 2949120 | tf_op jit(solution)/shard_map/reduce_scatter | solution.py:468
  534.6 556.0 %reduce-scatter.27.cloned.1.call-start = ((), (), s32[]{:S(2)}) async-start(), calls=%async_computation.26 | async-start | bytes 2949120 | tf_op jit(solution)/shard_map/reduce_scatter | solution.py:467
  983.6 44.6 %collective-permute-start.3 = (bf16[1024,768]{0,1:T(8,128)(2,1)}, bf16[1024,768]{0,1:T(8,128)(2,1)}, u32[]{:S(2)}, u32[]{:S(2)}) collective-permute-start(bf16[1024,768]{0,1:T(8,128)(2,1)} %bitcast.131), channel_id=1, source_target_pairs={{4,0},{5,1},{6,2},{7,3},{12,8},{13,9},{14,10},{15,11},{20,16},{21,... | collective-permute-start | bytes 4718600 | tf_op jit(solution)/shard_map/ppermute | solution.py:23
  1000.0 32.1 %collective-permute-start.4 = (bf16[1024,768]{0,1:T(8,128)(2,1)}, bf16[1024,768]{0,1:T(8,128)(2,1)}, u32[]{:S(2)}, u32[]{:S(2)}) collective-permute-start(bf16[1024,768]{0,1:T(8,128)(2,1)} %bitcast.141), channel_id=1, source_target_pairs={{4,0},{5,1},{6,2},{7,3},{12,8},{13,9},{14,10},{15,11},{20,16},{21,... | collective-permute-start | bytes 4718600 | tf_op jit(solution)/shard_map/ppermute | solution.py:23
  1044.2 96.1 %reduce-scatter.25.cloned.1.call-start = ((), (), s32[]{:S(2)}) async-start(), calls=%async_computation.25 | async-start | bytes 2949120 | tf_op jit(solution)/shard_map/reduce_scatter | solution.py:466
  1044.8 145.4 %reduce-scatter.23.cloned.1.call-start = ((), (), s32[]{:S(2)}) async-start(), calls=%async_computation.24 | async-start | bytes 2949120 | tf_op jit(solution)/shard_map/reduce_scatter | solution.py:465
  1045.6 258.1 %reduce-scatter.17.cloned.1.call-start = ((), (), s32[]{:S(2)}) async-start(), calls=%async_computation.21 | async-start | bytes 7864320 | tf_op jit(solution)/shard_map/reduce_scatter | solution.py:473
  1055.7 361.6 %reduce-scatter.19.cloned.1.call-start = ((), (), s32[]{:S(2)}) async-start(), calls=%async_computation.22 | async-start | bytes 7864320 | tf_op jit(solution)/shard_map/reduce_scatter | solution.py:474
  1065.6 465.1 %reduce-scatter.21.cloned.1.call-start = ((), (), s32[]{:S(2)}) async-start(), calls=%async_computation.23 | async-start | bytes 7864320 | tf_op jit(solution)/shard_map/reduce_scatter | solution.py:475
  1075.7 495.1 %reduce-scatter.35.cloned.1.call-start = ((), (), s32[]{:S(2)}) async-start(), calls=%async_computation.30 | async-start | bytes 491520
  1077.3 495.7 %reduce-scatter.33.cloned.1.call-start = ((), (), s32[]{:S(2)}) async-start(), calls=%async_computation.29 | async-start | bytes 491520
  1078.7 516.0 %reduce-scatter.31.cloned.1.call-start = ((), (), s32[]{:S(2)}) async-start(), calls=%async_computation.28 | async-start | bytes 491520
  1079.7 582.4 %all-reduce.22.cloned.1.call-start = ((), (), s32[]{:S(2)}) async-start(), calls=%async_computation.31 | async-start | bytes 4718592 | tf_op jit(solution)/shard_map/psum | solution.py:436
  1190.2 341.2 %copy-start.56 = (f32[1024,8]{0,1:T(8,128)S(1)}, f32[1024,8]{0,1:T(8,128)}, u32[]{:S(2)}) copy-start(f32[1024,8]{0,1:T(8,128)} %copy-done.55) | copy-start | bytes 98308
  1190.2 341.2 %copy-start.58 = (f32[1024,8]{0,1:T(8,128)S(1)}, f32[1024,8]{0,1:T(8,128)}, u32[]{:S(2)}) copy-start(f32[1024,8]{0,1:T(8,128)} %copy-done.57) | copy-start | bytes 98308
  1190.2 341.2 %copy-start.70 = (f32[1024]{0:T(1024)S(1)}, f32[1024]{0:T(1024)}, u32[]{:S(2)}) copy-start(f32[1024]{0:T(1024)} %copy-done.69) | copy-start | bytes 12292
  1190.2 504.9 %all-reduce.24.cloned.1.call-start = ((), (), s32[]{:S(2)}) async-start(), calls=%async_computation.32 | async-start | bytes 9437184 | tf_op jit(solution)/shard_map/psum | solution.py:477
  (115 other events, 1266.3 us)
Sparse Core Ops, SparseCore 0:
  9.6 30.8 all-gather.10
  42.1 29.8 all-gather.12
  73.6 29.5 all-gather.14
  104.6 29.5 all-gather.16
  135.6 62.1 all-gather.20
  199.2 62.1 all-gather.18
  263.0 62.1 all-gather.22
  534.7 48.4 reduce-scatter.28
  1044.3 46.2 reduce-scatter.26
  1092.7 47.5 reduce-scatter.24
  1142.6 47.5 reduce-scatter.22
  1192.3 111.2 reduce-scatter.16
  1306.0 111.2 reduce-scatter.18
  1419.4 111.2 reduce-scatter.20
  1533.4 17.6 reduce-scatter.34
  1554.0 19.0 reduce-scatter.32
  1575.7 18.8 reduce-scatter.30
  1598.4 63.7 all-reduce.21
  1664.9 30.1 all-reduce.23
where the time goes:
time: 1720 us; the launch traced here: 1710 us
  waiting for transfers between devices  561 us (33%)
  matrix products  464 us (27%)
  local copies, waits for them, and re-layouts  350 us (20%)
  other arithmetic  146 us (8%)
  blocking collectives  103 us (6%)
  loops' own time  37.2 us (2%)
  starting transfers between devices  34.2 us (2%)
    dot_general x6, matrix products, attend_back(): jnp.einsum('hqk,khd->qhd', grad_scores, key_blk, preferred_element_type=j...  116 us
    reduce_scatter x1, waiting for transfers between devices, on_device(): lax.psum_scatter(grad_up_w[None], 'dp', scatter_dimension=1, tiled=True)  114 us
    reduce_scatter x1, waiting for transfers between devices, on_device(): lax.psum_scatter(grad_down_w[None], 'dp', scatter_dimension=1, tiled=True)  113 us
    reduce_scatter x1, waiting for transfers between devices, on_device(): lax.psum_scatter(grad_gate_w[None], 'dp', scatter_dimension=1, tiled=True)  113 us
    dot_general x6, matrix products, attend_back(): jnp.einsum('hqk,qhd->khd', grad_scores, query_blk, preferred_element_type...  109 us
    unnamed x208, local copies, waits for them, and re-layouts  56.6 us
    dot_general x6, matrix products, contract_last(): lax.dot_general(left, right, (((1,), (1,)), ((), ())), preferred_element_...  50.5 us
    reduce_scatter x1, waiting for transfers between devices, on_device(): lax.psum_scatter(sum_query, 'dp', scatter_dimension=0, tiled=True)  49.9 us
  transfers between devices with their start and end apart: 28, of which 13 were waited for; matrix products, arithmetic and copies ran while one was open for 46% of the time, Pallas kernels for 0%

commit v1 on v0

v1 whole, which is shorter than its diff:
```python
import functools

import jax
import jax.numpy as jnp
import numpy as np
from jax import lax
from jax.experimental import pallas as pl
from jax.experimental.pallas import tpu as pltpu
from jax.sharding import PartitionSpec as P

HEADS = 12
HEAD_DIM = 64
WIN = 1024
NZ = 4
TQ = 256
TB = 256
FC = 256
LANES = 128
EPS = 1e-05
MASKED = -1000000000.0
HIGH = lax.Precision.HIGHEST
F32 = jnp.float32
BF16 = jnp.bfloat16
MIB = 1024 * 1024


def params(mib):
    return pltpu.CompilerParams(vmem_limit_bytes=mib * MIB)


def cost(flops, nbytes, trans=0):
    return pl.CostEstimate(flops=int(flops), bytes_accessed=int(nbytes), transcendentals=int(trans))


def dot(left, right):
    return jnp.dot(left, right, preferred_element_type=F32)


def dot_nt(left, right):
    return lax.dot_general(left, right, (((1,), (1,)), ((), ())), preferred_element_type=F32)


def dot_tn(left, right):
    return lax.dot_general(left, right, (((0,), (0,)), ((), ())), preferred_element_type=F32)


def iota(shape, axis):
    return lax.broadcasted_iota(jnp.int32, shape, axis)


def rope_tables(seq):
    half = HEAD_DIM // 2
    frequency = np.float32(10000.0) ** (
        -np.arange(half, dtype=np.float32) * np.float32(2.0) / np.float32(HEAD_DIM)
    )
    angles = np.arange(seq, dtype=np.float32)[:, None] * frequency.astype(np.float32)[None, :]
    cos = np.cos(angles.astype(np.float64)).astype(np.float32)
    sin = np.sin(angles.astype(np.float64)).astype(np.float32)
    return np.concatenate([cos] * 4, axis=1), np.concatenate([-sin, sin, -sin, sin], axis=1)


def swap_halves(chunk):
    lane = iota(chunk.shape, 1)
    return jnp.where(
        lane % HEAD_DIM < HEAD_DIM // 2, pltpu.roll(chunk, 96, 1), pltpu.roll(chunk, 32, 1)
    )


def place_kernel(experts, cap, routes_ref, rank_col_ref, rank_row_ref, flat_ref, flat_t_ref):
    rows = routes_ref.shape[0]
    lane = iota((rows, LANES), 1)
    first, second = routes_ref[:, 0:1], routes_ref[:, 1:2]
    hot_first, hot_second = first == lane, second == lane
    hot = (hot_first.astype(F32) + hot_second.astype(F32)).astype(BF16)
    earlier = jnp.where(rank_row_ref[...] < rank_col_ref[...], 1.0, 0.0).astype(BF16)
    counts = dot(earlier, hot)

    def flat(hit, route):
        slot = jnp.sum(jnp.where(hit, counts, 0.0), axis=1, keepdims=True).astype(jnp.int32)
        return jnp.where((route < experts) & (slot < cap), route * cap + slot, experts * cap)

    out = jnp.where(
        lane == 0, flat(hot_first, first), jnp.where(lane == 1, flat(hot_second, second), 0)
    )
    flat_ref[...] = out
    flat_t_ref[...] = out.astype(F32).T[:8]


def place(routes, ranks, experts, cap):
    rows = routes.shape[0]
    return pl.pallas_call(
        functools.partial(place_kernel, experts, cap),
        out_shape=(
            jax.ShapeDtypeStruct((rows, LANES), jnp.int32),
            jax.ShapeDtypeStruct((8, rows), F32),
        ),
        compiler_params=params(32),
        cost_estimate=cost(2 * rows * rows * LANES, 8 * rows * LANES),
        name="place",
    )(routes, ranks.reshape(rows, 1), ranks.reshape(1, rows))


def qkv_kernel(ctx_ref, x_ref, gain_ref, w_ref, cos_ref, sin_ref, out_ref, aone_ref):
    width = x_ref.shape[1]
    values = x_ref[...].astype(F32)
    scale = lax.rsqrt(jnp.mean(values * values, axis=-1, keepdims=True) + EPS)
    normed = (values * scale * gain_ref[...]).astype(BF16)
    aone_ref[...] = normed
    cos, sin = cos_ref[...], sin_ref[...]
    pairs = width // LANES
    for which in range(3):
        product = dot(normed, w_ref[which])
        for pair in range(pairs):
            chunk = product[:, pair * LANES : (pair + 1) * LANES]
            if which < 2:
                chunk = chunk * cos + swap_halves(chunk) * sin
            if which == 0:
                chunk = chunk * HEAD_DIM ** (-0.5)
            side, place_in = pair // (pairs // 2), pair % (pairs // 2)
            out_ref[side, which, :, place_in * LANES : (place_in + 1) * LANES] = chunk.astype(BF16)


def project(ctx, x, gain, w_qkv, cos, sin):
    rows, width = x.shape
    blocks = rows // TB
    return pl.pallas_call(
        qkv_kernel,
        grid_spec=pltpu.PrefetchScalarGridSpec(
            num_scalar_prefetch=1,
            grid=(blocks,),
            in_specs=[
                pl.BlockSpec((TB, width), lambda i, c: (i, 0)),
                pl.BlockSpec((1, width), lambda i, c: (0, 0)),
                pl.BlockSpec((3, width, width), lambda i, c: (0, 0, 0)),
                pl.BlockSpec((TB, LANES), lambda i, c: (c[0] * blocks + i, 0)),
                pl.BlockSpec((TB, LANES), lambda i, c: (c[0] * blocks + i, 0)),
            ],
            out_specs=[
                pl.BlockSpec((2, 3, TB, width // 2), lambda i, c: (0, 0, i, 0)),
                pl.BlockSpec((TB, width), lambda i, c: (i, 0)),
            ],
        ),
        out_shape=(
            jax.ShapeDtypeStruct((2, 3, rows, width // 2), BF16),
            jax.ShapeDtypeStruct((rows, width), BF16),
        ),
        compiler_params=params(40),
        cost_estimate=cost(6 * rows * width * width, 6 * width * width + 12 * rows * width),
        name="project",
    )(ctx, x, gain, w_qkv, cos, sin)


def head_masks():
    lane = iota((TQ, LANES), 1)
    low = jnp.where(lane < HEAD_DIM, 1.0, 0.0).astype(BF16)
    return low, (1.0 - low.astype(F32)).astype(BF16)


def attend_kernel(first_ref, q_ref, k_ref, v_ref, lo_ref, o_ref, lse_ref, vt_ref):
    per = q_ref.shape[2] // TQ
    count = 2 * per
    masks = head_masks()
    sub = iota((TQ, TQ), 0)
    diagonal = sub <= iota((TQ, TQ), 1)

    def turn(tile, carry):
        vt_ref[tile] = v_ref[tile // per, 0, pl.ds((tile % per) * TQ, TQ), :].T
        return carry

    lax.fori_loop(0, count, turn, 0)

    def q_step(qi, carry):
        rows = pl.ds((qi % per) * TQ, TQ)
        query = q_ref[qi // per, 0, rows, :]
        queries = [query * mask for mask in masks]
        low = lo_ref[qi]
        keys = k_ref[qi // per, 0, rows, :]
        turned = vt_ref[qi]
        ok = diagonal & (sub >= low - qi * TQ)
        state = []
        for head in range(2):
            scores = jnp.where(ok, dot_nt(keys, queries[head]), MASKED)
            peak = jnp.max(scores, axis=0, keepdims=True)
            probs = jnp.exp(scores - peak)
            total = jnp.sum(probs, axis=0, keepdims=True)
            mixed = dot(turned[head * HEAD_DIM : (head + 1) * HEAD_DIM], probs.astype(BF16))
            state += [peak, total, mixed]

        def k_step(ki, state):
            keys = k_ref[ki // per, 0, pl.ds((ki % per) * TQ, TQ), :]
            turned = vt_ref[ki]
            ok = sub >= low - ki * TQ
            new = []
            for head in range(2):
                peak, total, mixed = state[3 * head : 3 * head + 3]
                scores = jnp.where(ok, dot_nt(keys, queries[head]), MASKED)
                top = jnp.maximum(peak, jnp.max(scores, axis=0, keepdims=True))
                shrink = jnp.exp(peak - top)
                probs = jnp.exp(scores - top)
                total = total * shrink + jnp.sum(probs, axis=0, keepdims=True)
                part = dot(turned[head * HEAD_DIM : (head + 1) * HEAD_DIM], probs.astype(BF16))
                new += [top, total, mixed * shrink + part]
            return tuple(new)

        state = lax.fori_loop(first_ref[qi], qi, k_step, tuple(state))
        out = jnp.concatenate([state[2] / state[1], state[5] / state[4]], axis=0)
        o_ref[qi // per, rows, :] = out.T.astype(BF16)
        lse_ref[0, qi, 0:1, :] = state[0] + jnp.log(state[1])
        lse_ref[0, qi, 1:2, :] = state[3] + jnp.log(state[4])
        return carry

    lax.fori_loop(0, count, q_step, 0)


def part_spec(which, rows):
    return pl.BlockSpec((2, 1, rows, LANES), lambda p, first, which=which: (0, which, 0, p))


def attend(first, qkv, low):
    _, _, rows, half = qkv.shape
    pairs = half // LANES
    tiles = 2 * rows // TQ
    return pl.pallas_call(
        attend_kernel,
        grid_spec=pltpu.PrefetchScalarGridSpec(
            num_scalar_prefetch=1,
            grid=(pairs,),
            in_specs=[
                part_spec(0, rows),
                part_spec(1, rows),
                part_spec(2, rows),
                pl.BlockSpec((tiles, 1, TQ), lambda p, first: (0, 0, 0)),
            ],
            out_specs=[
                pl.BlockSpec((2, rows, LANES), lambda p, first: (0, 0, p)),
                pl.BlockSpec((1, tiles, 8, TQ), lambda p, first: (p, 0, 0, 0)),
            ],
            scratch_shapes=[pltpu.VMEM((tiles, LANES, TQ), BF16)],
        ),
        out_shape=(
            jax.ShapeDtypeStruct((2, rows, half), BF16),
            jax.ShapeDtypeStruct((pairs, tiles, 8, TQ), F32),
        ),
        compiler_params=params(40),
        cost_estimate=cost(40e9, 16 * rows * half, 12e6),
        name="attend",
    )(first, qkv, qkv, qkv, low)


def attend_back_kernel(
    first_ref,
    q_ref,
    k_ref,
    v_ref,
    do_ref,
    o_ref,
    lse_ref,
    lo_ref,
    cos_ref,
    sin_ref,
    g_ref,
    kt_ref,
    delta_ref,
    dk_ref,
    dv_ref,
):
    per = q_ref.shape[2] // TQ
    count = 2 * per
    masks = head_masks()
    sub = iota((TQ, TQ), 0)
    diagonal = sub <= iota((TQ, TQ), 1)

    def prepare(tile, carry):
        rows = pl.ds((tile % per) * TQ, TQ)
        kt_ref[tile] = k_ref[tile // per, 0, rows, :].T
        both = o_ref[tile // per, rows, :].astype(F32) * do_ref[tile // per, rows, :].astype(F32)
        both = both.T
        delta_ref[tile, 0:1, :] = jnp.sum(both[:HEAD_DIM], axis=0, keepdims=True)
        delta_ref[tile, 1:2, :] = jnp.sum(both[HEAD_DIM:], axis=0, keepdims=True)
        dk_ref[tile] = jnp.zeros((TQ, LANES), F32)
        dv_ref[tile] = jnp.zeros((TQ, LANES), F32)
        return carry

    lax.fori_loop(0, count, prepare, 0)

    def q_step(qi, carry):
        rows = pl.ds((qi % per) * TQ, TQ)
        query = q_ref[qi // per, 0, rows, :]
        grad = do_ref[qi // per, rows, :]
        queries = [query * mask for mask in masks]
        grads = [grad * mask for mask in masks]
        both_queries = jnp.concatenate(queries, axis=0)
        both_grads = jnp.concatenate(grads, axis=0)
        low = lo_ref[qi]
        lse = [lse_ref[0, qi, h : h + 1, :] for h in range(2)]
        delta = [delta_ref[qi, h : h + 1, :] for h in range(2)]

        def tile(ki, ok, sums):
            at = pl.ds((ki % per) * TQ, TQ)
            keys = k_ref[ki // per, 0, at, :]
            values = v_ref[ki // per, 0, at, :]
            turned = kt_ref[ki]
            all_probs, all_scores, new = [], [], []
            for h in range(2):
                scores = jnp.where(ok, dot_nt(keys, queries[h]), MASKED)
                probs = jnp.exp(scores - lse[h])
                grad_probs = dot_nt(values, grads[h])
                grad_scores = (probs * (grad_probs - delta[h])).astype(BF16)
                new.append(
                    sums[h] + dot(turned[h * HEAD_DIM : (h + 1) * HEAD_DIM], grad_scores)
                )
                all_probs.append(probs.astype(BF16))
                all_scores.append(grad_scores)
            dv_ref[ki] += dot(jnp.concatenate(all_probs, axis=1), both_grads)
            dk_ref[ki] += dot(jnp.concatenate(all_scores, axis=1), both_queries)
            return tuple(new)

        start = jnp.zeros((HEAD_DIM, TQ), F32)
        sums = tile(qi, diagonal & (sub >= low - qi * TQ), (start, start))
        sums = lax.fori_loop(
            first_ref[qi], qi, lambda ki, s: tile(ki, sub >= low - ki * TQ, s), sums
        )
        grad_query = jnp.concatenate(sums, axis=0).T * HEAD_DIM ** (-0.5)
        cos, sin = cos_ref[qi // per, rows, :], sin_ref[qi // per, rows, :]
        g_ref[qi // per, 0, rows, :] = (grad_query * cos - swap_halves(grad_query) * sin).astype(
            BF16
        )
        return carry

    lax.fori_loop(0, count, q_step, 0)

    def finish(tile, carry):
        rows = pl.ds((tile % per) * TQ, TQ)
        cos, sin = cos_ref[tile // per, rows, :], sin_ref[tile // per, rows, :]
        grad_key = dk_ref[tile]
        g_ref[tile // per, 1, rows, :] = (grad_key * cos - swap_halves(grad_key) * sin).astype(BF16)
        g_ref[tile // per, 2, rows, :] = dv_ref[tile].astype(BF16)
        return carry

    lax.fori_loop(0, count, finish, 0)


def attend_back(first, qkv, grad_o, o, lse, low, cos, sin):
    _, _, rows, half = qkv.shape
    pairs = half // LANES
    tiles = 2 * rows // TQ
    side = pl.BlockSpec((2, rows, LANES), lambda p, first: (0, 0, p))
    table = pl.BlockSpec((2, rows, LANES), lambda p, first: (0, 0, 0))
    return pl.pallas_call(
        attend_back_kernel,
        grid_spec=pltpu.PrefetchScalarGridSpec(
            num_scalar_prefetch=1,
            grid=(pairs,),
            in_specs=[
                part_spec(0, rows),
                part_spec(1, rows),
                part_spec(2, rows),
                side,
                side,
                pl.BlockSpec((1, tiles, 8, TQ), lambda p, first: (p, 0, 0, 0)),
                pl.BlockSpec((tiles, 1, TQ), lambda p, first: (0, 0, 0)),
                table,
                table,
            ],
            out_specs=pl.BlockSpec((2, 3, rows, LANES), lambda p, first: (0, 0, 0, p)),
            scratch_shapes=[
                pltpu.VMEM((tiles, LANES, TQ), BF16),
                pltpu.VMEM((tiles, 8, TQ), F32),
                pltpu.VMEM((tiles, TQ, LANES), F32),
                pltpu.VMEM((tiles, TQ, LANES), F32),
            ],
        ),
        out_shape=jax.ShapeDtypeStruct((2, 3, rows, half), BF16),
        compiler_params=params(48),
        cost_estimate=cost(100e9, 32 * rows * half, 12e6),
        name="attend_back",
    )(first, qkv, qkv, qkv, grad_o, o, lse, low, cos, sin)


def middle_kernel(
    total, x_ref, o_ref, w_ref, gain_ref, route_ref, prev_ref, routes_ref, hres_ref, atwo_ref, stat_ref
):
    half = o_ref.shape[2]
    hres = (
        x_ref[...].astype(F32) + dot(o_ref[0], w_ref[:half]) + dot(o_ref[1], w_ref[half:])
    )
    hres_ref[...] = hres
    scale = lax.rsqrt(jnp.mean(hres * hres, axis=-1, keepdims=True) + EPS)
    atwo = (hres * scale * gain_ref[...]).astype(BF16)
    atwo_ref[...] = atwo
    logits = dot(atwo, route_ref[...]) + prev_ref[...]
    lane = iota(logits.shape, 1)

    def soft(inside):
        peak = jnp.max(jnp.where(inside, logits, -jnp.inf), axis=1, keepdims=True)
        powers = jnp.where(inside, jnp.exp(jnp.where(inside, logits - peak, 0.0)), 0.0)
        return powers / jnp.sum(powers, axis=1, keepdims=True)

    probs = soft(lane < total)
    stat = probs
    for j in range(2):
        start = total + 2 * j
        stat = stat + soft((lane >= start) & (lane < start + 2))
    stat = jnp.where(lane == total + 4, scale, stat)
    for k in range(2):
        gate = jnp.sum(
            jnp.where(lane == routes_ref[:, k : k + 1], probs, 0.0), axis=1, keepdims=True
        )
        stat = jnp.where(lane == total + 5 + k, gate, stat)
    stat_ref[...] = stat


def middle(total, x, o, w_out, gain, route_w, prev, routes):
    rows, width = x.shape
    token = lambda i: (i, 0)
    whole = lambda i: (0, 0)
    return pl.pallas_call(
        functools.partial(middle_kernel, total),
        grid=(rows // TB,),
        in_specs=[
            pl.BlockSpec((TB, width), token),
            pl.BlockSpec((2, TB, width // 2), lambda i: (0, i, 0)),
            pl.BlockSpec((width, width), whole),
            pl.BlockSpec((1, width), whole),
            pl.BlockSpec((width, LANES), whole),
            pl.BlockSpec((TB, LANES), token),
            pl.BlockSpec((TB, 2), token),
        ],
        out_specs=[
            pl.BlockSpec((TB, width), token),
            pl.BlockSpec((TB, width), token),
            pl.BlockSpec((TB, LANES), token),
        ],
        out_shape=(
            jax.ShapeDtypeStruct((rows, width), F32),
            jax.ShapeDtypeStruct((rows, width), BF16),
            jax.ShapeDtypeStruct((rows, LANES), F32),
        ),
        compiler_params=params(40),
        cost_estimate=cost(2 * rows * width * width, 2 * width * width + 10 * rows * width),
        name="middle",
    )(x, o, w_out, gain, route_w, prev, routes)


def dispatch_kernel(total, flat_ref, atwo_ref, dy_ref, stat_ref, rows_ref, grads_ref):
    cap = rows_ref.shape[1]
    tokens = atwo_ref.shape[0]
    slot = (iota((cap, tokens), 0) + pl.program_id(0) * cap).astype(F32)
    gates = stat_ref[...].T
    first, second = flat_ref[0:1, :] == slot, flat_ref[1:2, :] == slot
    hot = jnp.where(first | second, 1.0, 0.0).astype(BF16)
    gate = jnp.sum(
        jnp.where(first, gates[total + 5 : total + 6], 0.0)
        + jnp.where(second, gates[total + 6 : total + 7], 0.0),
        axis=1,
        keepdims=True,
    )
    rows_ref[0] = dot(hot, atwo_ref[...]).astype(BF16)
    grads_ref[0] = (dot(hot, dy_ref[...]) * gate).astype(BF16)


def dispatch(total, experts, cap, flat_t, atwo, dy, stat):
    rows, width = atwo.shape
    whole = lambda e: (0, 0)
    return pl.pallas_call(
        functools.partial(dispatch_kernel, total),
        grid=(experts,),
        in_specs=[
            pl.BlockSpec((8, rows), whole),
            pl.BlockSpec((rows, width), whole),
            pl.BlockSpec((rows, width), whole),
            pl.BlockSpec((rows, LANES), whole),
        ],
        out_specs=[pl.BlockSpec((1, cap, width), lambda e: (e, 0, 0))] * 2,
        out_shape=(jax.ShapeDtypeStruct((experts, cap, width), BF16),) * 2,
        compiler_params=params(40),
        cost_estimate=cost(4 * experts * cap * rows * width, 8 * rows * width),
        name="dispatch",
    )(flat_t, atwo, dy, stat)


def up_kernel(x_ref, wg_ref, wu_ref, wd_ref, flow_ref, z_ref, a_ref, b_ref, acc_ref):
    step = pl.program_id(0)
    rows = x_ref[...]
    gate = dot(rows, wg_ref[0])
    up = dot(rows, wu_ref[0])
    sig = 1.0 / (1.0 + jnp.exp(-gate))
    swish = gate * sig
    hidden = (swish * up).astype(BF16)
    z_ref[...] = hidden
    a_ref[...] = (up * sig * (1.0 + gate * (1.0 - sig))).astype(BF16)
    b_ref[...] = swish.astype(BF16)
    part = dot(hidden, jnp.concatenate([wd_ref[0], wd_ref[1]], axis=1))

    @pl.when(step == 0)
    def _():
        acc_ref[...] = part

    @pl.when(step > 0)
    def _():
        acc_ref[...] += part

    @pl.when(step == pl.num_programs(0) - 1)
    def _():
        flow_ref[...] = acc_ref[...].astype(BF16)


def weight_specs(width, hidden):
    chunks = hidden // 2 // FC
    wide = pl.BlockSpec((1, width, FC), lambda f: (f // chunks, 0, f % chunks))
    down = pl.BlockSpec((2, FC, width // 2), lambda f: (0, f, 0))
    return wide, down


def expert_up(x, wg, wu, wd):
    rows, width = x.shape
    hidden = wd.shape[1]
    wide, down = weight_specs(width, hidden)
    whole = pl.BlockSpec((rows, width), lambda f: (0, 0))
    chunk = pl.BlockSpec((rows, FC), lambda f: (0, f))
    return pl.pallas_call(
        up_kernel,
        grid=(hidden // FC,),
        in_specs=[whole, wide, wide, down],
        out_specs=[whole, chunk, chunk, chunk],
        out_shape=(
            jax.ShapeDtypeStruct((rows, width), BF16),
            jax.ShapeDtypeStruct((rows, hidden), BF16),
            jax.ShapeDtypeStruct((rows, hidden), BF16),
            jax.ShapeDtypeStruct((rows, hidden), BF16),
        ),
        scratch_shapes=[pltpu.VMEM((rows, width), F32)],
        compiler_params=params(48),
        cost_estimate=cost(6 * rows * width * hidden, 6 * width * hidden + 6 * rows * hidden, rows * hidden),
        name="expert_up",
    )(x, wg, wu, wd)


def down_kernel(dflow_ref, wg_ref, wu_ref, wd_ref, a_ref, b_ref, drow_ref, dg_ref, du_ref, acc_ref):
    step = pl.program_id(0)
    dz = dot_nt(dflow_ref[...], jnp.concatenate([wd_ref[0], wd_ref[1]], axis=1))
    dg = (dz * a_ref[...].astype(F32)).astype(BF16)
    du = (dz * b_ref[...].astype(F32)).astype(BF16)
    dg_ref[...] = dg
    du_ref[...] = du
    part = dot_nt(dg, wg_ref[0]) + dot_nt(du, wu_ref[0])

    @pl.when(step == 0)
    def _():
        acc_ref[...] = part

    @pl.when(step > 0)
    def _():
        acc_ref[...] += part

    @pl.when(step == pl.num_programs(0) - 1)
    def _():
        drow_ref[...] = acc_ref[...].astype(BF16)


def expert_down(dflow, wg, wu, wd, a, b):
    rows, width = dflow.shape
    hidden = wd.shape[1]
    wide, down = weight_specs(width, hidden)
    whole = pl.BlockSpec((rows, width), lambda f: (0, 0))
    chunk = pl.BlockSpec((rows, FC), lambda f: (0, f))
    return pl.pallas_call(
        down_kernel,
        grid=(hidden // FC,),
        in_specs=[whole, wide, wide, down, chunk, chunk],
        out_specs=[whole, chunk, chunk],
        out_shape=(
            jax.ShapeDtypeStruct((rows, width), BF16),
            jax.ShapeDtypeStruct((rows, hidden), BF16),
            jax.ShapeDtypeStruct((rows, hidden), BF16),
        ),
        scratch_shapes=[pltpu.VMEM((rows, width), F32)],
        compiler_params=params(48),
        cost_estimate=cost(6 * rows * width * hidden, 6 * width * hidden + 8 * rows * hidden),
        name="expert_down",
    )(dflow, wg, wu, wd, a, b)


def wgrad_kernel(x_ref, dflow_ref, z_ref, dg_ref, du_ref, gg_ref, gu_ref, gd_ref, xt_ref):
    @pl.when(pl.program_id(0) == 0)
    def _():
        xt_ref[...] = x_ref[...].T

    turned = xt_ref[...]
    gg_ref[0] = dot(turned, dg_ref[...]).astype(BF16)
    gu_ref[0] = dot(turned, du_ref[...]).astype(BF16)
    down = dot(z_ref[...].T, dflow_ref[...]).astype(BF16)
    half = down.shape[1] // 2
    gd_ref[0] = down[:, :half]
    gd_ref[1] = down[:, half:]


def expert_wgrad(x, dflow, z, dg, du):
    rows, width = x.shape
    hidden = z.shape[1]
    wide, down = weight_specs(width, hidden)
    whole = pl.BlockSpec((rows, width), lambda f: (0, 0))
    chunk = pl.BlockSpec((rows, FC), lambda f: (0, f))
    return pl.pallas_call(
        wgrad_kernel,
        grid=(hidden // FC,),
        in_specs=[whole, whole, chunk, chunk, chunk],
        out_specs=[wide, wide, down],
        out_shape=(
            jax.ShapeDtypeStruct((2, width, hidden // 2), BF16),
            jax.ShapeDtypeStruct((2, width, hidden // 2), BF16),
            jax.ShapeDtypeStruct((2, hidden, width // 2), BF16),
        ),
        scratch_shapes=[pltpu.VMEM((width, rows), BF16)],
        compiler_params=params(48),
        cost_estimate=cost(6 * rows * width * hidden, 6 * width * hidden + 6 * rows * hidden),
        name="expert_wgrad",
    )(x, dflow, z, dg, du)


def combine_kernel(
    experts,
    total,
    flow_ref,
    drow_ref,
    flat_ref,
    stat_ref,
    routes_ref,
    hres_ref,
    atwo_ref,
    dy_ref,
    o_ref,
    vec_ref,
    gain_ref,
    route_ref,
    w_ref,
    out_ref,
    dh_ref,
    dolow_ref,
    dlogit_ref,
    gw_ref,
    small_ref,
):
    step = pl.program_id(0)
    slots = flow_ref.shape[0]
    half = o_ref.shape[2]
    gain = gain_ref[...]
    stat = stat_ref[...]
    hres = hres_ref[...]
    dy = dy_ref[...].astype(F32)
    scale = stat[:, total + 4 : total + 5]
    gates = [stat[:, total + 5 + k : total + 6 + k] for k in range(2)]
    ntwo = hres * scale * gain
    spread = iota((TB, slots), 1)
    hots = [flat_ref[:, k : k + 1] == spread for k in range(2)]
    returned = flow_ref[...]
    mixes = [[stat[:, total + 2 * j + i : total + 2 * j + i + 1] for i in range(2)] for j in range(2)]
    vecs = [vec_ref[j : j + 1, :] for j in range(2)]
    moe = jnp.zeros_like(hres)
    lane = iota((TB, LANES), 1)
    dpgate = jnp.zeros((TB, LANES), F32)
    weight = jnp.zeros((TB, 1), F32)
    const_weights = [jnp.zeros((TB, 1), F32)] * 2
    for k in range(2):
        route = routes_ref[:, k : k + 1]
        epair = dot(jnp.where(hots[k], 1.0, 0.0).astype(BF16), returned)
        share = jnp.where(route == experts + 1, 1.0, 0.0)
        weight = weight + share * gates[k]
        for j in range(2):
            chosen = jnp.where(route == experts + 2 + j, 1.0, 0.0)
            share = share + chosen * mixes[j][0]
            epair = epair + (chosen * mixes[j][1]) * vecs[j]
            const_weights[j] = const_weights[j] + chosen * gates[k]
        epair = epair + share * ntwo
        moe = moe + gates[k] * epair
        dgate = jnp.sum(dy * epair, axis=1, keepdims=True)
        dpgate = dpgate + jnp.where(lane == route, dgate, 0.0)
    out_ref[...] = (hres + moe).astype(BF16)

    pgate = jnp.where(lane < total, stat, 0.0)
    dlogit = pgate * (dpgate - jnp.sum(pgate * dpgate, axis=1, keepdims=True))
    dlogit_ref[...] = dlogit
    dot_normed = jnp.sum(dy * ntwo, axis=1, keepdims=True)
    droute = dlogit
    vec_rows = []
    for j in range(2):
        dot_vec = jnp.sum(dy * vecs[j], axis=1, keepdims=True)
        grads = [const_weights[j] * dot_normed, const_weights[j] * dot_vec]
        inner = mixes[j][0] * grads[0] + mixes[j][1] * grads[1]
        for i in range(2):
            droute = jnp.where(
                lane == total + 2 * j + i, mixes[j][i] * (grads[i] - inner), droute
            )
        weight = weight + const_weights[j] * mixes[j][0]
        vec_rows.append(jnp.sum((const_weights[j] * mixes[j][1]) * dy, axis=0, keepdims=True))
    droute = droute.astype(BF16)
    hot_any = jnp.where(hots[0] | hots[1], 1.0, 0.0).astype(BF16)
    dntwo = weight * dy + dot_nt(droute, route_ref[...]) + dot(hot_any, drow_ref[...])
    turned = dntwo * gain
    inner = jnp.mean(hres * turned, axis=1, keepdims=True)
    dh = dy + scale * turned - hres * (scale * scale * scale * inner)
    dh_ref[...] = dh
    dhlow = dh.astype(BF16)
    dolow = dot_nt(dhlow, w_ref[...]).astype(BF16)
    dolow_ref[0] = dolow[:, :half]
    dolow_ref[1] = dolow[:, half:]
    gain_row = jnp.sum(dntwo * hres * scale, axis=0, keepdims=True)
    route_rows = dot(droute.T, atwo_ref[...])
    fill = small_ref.shape[0] - total - 7
    small = jnp.concatenate(
        [route_rows[: total + 4], gain_row, vec_rows[0], vec_rows[1], jnp.zeros((fill, hres.shape[1]), F32)],
        axis=0,
    )
    parts = [dot(o_ref[i].T, dhlow) for i in range(2)]

    @pl.when(step == 0)
    def _():
        small_ref[...] = small
        gw_ref[:half] = parts[0]
        gw_ref[half:] = parts[1]

    @pl.when(step > 0)
    def _():
        small_ref[...] += small
        gw_ref[:half] += parts[0]
        gw_ref[half:] += parts[1]


def combine(experts, total, flow, drow, flat, stat, routes, hres, atwo, dy, o, vec, gain, route_w, w_out):
    rows, width = hres.shape
    slots = flow.shape[0]
    token = lambda i: (i, 0)
    whole = lambda i: (0, 0)
    side = pl.BlockSpec((2, TB, width // 2), lambda i: (0, i, 0))
    small_rows = -(-(total + 7) // 8) * 8
    return pl.pallas_call(
        functools.partial(combine_kernel, experts, total),
        grid=(rows // TB,),
        in_specs=[
            pl.BlockSpec((slots, width), whole),
            pl.BlockSpec((slots, width), whole),
            pl.BlockSpec((TB, LANES), token),
            pl.BlockSpec((TB, LANES), token),
            pl.BlockSpec((TB, 2), token),
            pl.BlockSpec((TB, width), token),
            pl.BlockSpec((TB, width), token),
            pl.BlockSpec((TB, width), token),
            side,
            pl.BlockSpec((2, width), whole),
            pl.BlockSpec((1, width), whole),
            pl.BlockSpec((width, LANES), whole),
            pl.BlockSpec((width, width), whole),
        ],
        out_specs=[
            pl.BlockSpec((TB, width), token),
            pl.BlockSpec((TB, width), token),
            side,
            pl.BlockSpec((TB, LANES), token),
            pl.BlockSpec((width, width), whole),
            pl.BlockSpec((small_rows, width), whole),
        ],
        out_shape=(
            jax.ShapeDtypeStruct((rows, width), BF16),
            jax.ShapeDtypeStruct((rows, width), F32),
            jax.ShapeDtypeStruct((2, rows, width // 2), BF16),
            jax.ShapeDtypeStruct((rows, LANES), F32),
            jax.ShapeDtypeStruct((width, width), F32),
            jax.ShapeDtypeStruct((small_rows, width), F32),
        ),
        compiler_params=params(56),
        cost_estimate=cost(
            6 * rows * slots * width + 4 * rows * width * width, 30 * rows * width + 8 * width * width
        ),
        name="combine",
    )(flow, drow, flat, stat, routes, hres, atwo, dy, o, vec, gain, route_w, w_out)


def project_back_kernel(g_ref, w_ref, x_ref, aone_ref, dh_ref, gain_ref, out_ref, gw_ref, gain_out_ref):
    step = pl.program_id(0)
    half = g_ref.shape[3]
    turned = aone_ref[...].T
    dnone = None
    for which in range(3):
        grad = jnp.concatenate([g_ref[0, which], g_ref[1, which]], axis=1)
        part = dot_nt(grad, w_ref[which])
        dnone = part if dnone is None else dnone + part
        weight = dot(turned, grad)

        @pl.when(step == 0)
        def _():
            gw_ref[which] = weight

        @pl.when(step > 0)
        def _():
            gw_ref[which] += weight

    values = x_ref[...].astype(F32)
    scale = lax.rsqrt(jnp.mean(values * values, axis=-1, keepdims=True) + EPS)
    scaled = dnone * gain_ref[...]
    inner = jnp.mean(values * scaled, axis=1, keepdims=True)
    out_ref[...] = dh_ref[...] + scale * scaled - values * (scale * scale * scale * inner)
    row = jnp.sum(dnone * values * scale, axis=0, keepdims=True)

    @pl.when(step == 0)
    def _():
        gain_out_ref[...] = row

    @pl.when(step > 0)
    def _():
        gain_out_ref[...] += row


def project_back(grad, w_qkv, x, aone, dh, gain):
    rows, width = x.shape
    token = lambda i: (i, 0)
    whole = lambda i: (0, 0)
    return pl.pallas_call(
        project_back_kernel,
        grid=(rows // TB,),
        in_specs=[
            pl.BlockSpec((2, 3, TB, width // 2), lambda i: (0, 0, i, 0)),
            pl.BlockSpec((3, width, width), lambda i: (0, 0, 0)),
            pl.BlockSpec((TB, width), token),
            pl.BlockSpec((TB, width), token),
            pl.BlockSpec((TB, width), token),
            pl.BlockSpec((1, width), whole),
        ],
        out_specs=[
            pl.BlockSpec((TB, width), token),
            pl.BlockSpec((3, width, width), lambda i: (0, 0, 0)),
            pl.BlockSpec((1, width), whole),
        ],
        out_shape=(
            jax.ShapeDtypeStruct((rows, width), F32),
            jax.ShapeDtypeStruct((3, width, width), F32),
            jax.ShapeDtypeStruct((1, width), F32),
        ),
        compiler_params=params(56),
        cost_estimate=cost(12 * rows * width * width, 18 * width * width + 20 * rows * width),
        name="project_back",
    )(grad, w_qkv, x, aone, dh, gain)


def swap_cores(value):
    return lax.all_to_all(value, "context", split_axis=0, concat_axis=0, tiled=True)


def swap_experts(value):
    return lax.all_to_all(value, "expert", split_axis=0, concat_axis=0, tiled=True)


def gather_half(shard, width):
    core = lax.axis_index("context")
    mine = lax.dynamic_slice_in_dim(shard, core * width, width, 1)
    whole = lax.all_gather(mine, ("context", "dp"), axis=0)
    dp = lax.axis_size("dp")
    return whole.reshape(2, dp * mine.shape[0], width)


def on_device(
    tokens,
    segments,
    routes,
    prev_logits,
    ranks,
    cotangent,
    norm_one,
    w_query,
    w_key,
    w_value,
    w_out,
    norm_two,
    router,
    w_res,
    const_mix,
    const_vec,
    w_gate,
    w_up,
    w_down,
):
    experts = lax.axis_size("expert")
    dp = lax.axis_size("dp")
    total = experts + NZ
    _, rows, width = tokens.shape
    hidden = w_gate.shape[2]
    cap = (18 * rows + 8 * total - 1) // (8 * total)
    seq = 2 * rows
    tiles = seq // TQ
    core = lax.axis_index("context")
    mesh_axes = ("expert", "context", "dp")

    w_qkv = lax.all_gather(jnp.stack([w_query, w_key, w_value]), "dp", axis=1, tiled=True)
    extra = jnp.concatenate(
        [
            norm_one.astype(BF16)[:, None],
            norm_two.astype(BF16)[:, None],
            const_vec,
            router,
            const_mix,
        ],
        axis=1,
    )
    extra = jnp.pad(extra, ((0, 0), (0, LANES - extra.shape[1])))
    out_and_extra = lax.all_gather(
        jnp.concatenate([w_out, extra], axis=1), "dp", axis=0, tiled=True
    )
    out_w = out_and_extra[:, :width]
    extra = out_and_extra[:, width:]
    extra_t = extra[:, :4].astype(F32).T
    gain_one, gain_two, vec = extra_t[0:1], extra_t[1:2], extra_t[2:4]
    route_w = jnp.pad(extra[:, 4 : 8 + total], ((0, 0), (0, LANES - total - 4)))

    gate_w = gather_half(w_gate[0], hidden // 2)
    up_w = gather_half(w_up[0], hidden // 2)
    down_w = gather_half(w_down[0], width // 2)

    flat, flat_t = place(routes[0], ranks[0, 0], experts, cap)
    segs = lax.all_gather(segments[0], "context", axis=0, tiled=True)
    places = jnp.arange(seq, dtype=jnp.int32)
    starts = jnp.sum((segs[None, :] < segs[:, None]).astype(jnp.int32), axis=1)
    low = jnp.maximum(starts, places - (WIN - 1)).reshape(tiles, 1, TQ)
    first = low[:, 0, 0] // TQ
    cos, sin = rope_tables(seq)
    cos, sin = jnp.asarray(cos), jnp.asarray(sin)
    prev_term = jnp.pad(
        jnp.dot(prev_logits[0], w_res.astype(F32), precision=HIGH),
        ((0, 0), (0, LANES - total)),
    )

    x = tokens[0]
    dy = cotangent[0]
    sent, aone = project(core.reshape(1), x, gain_one, w_qkv, cos, sin)
    qkv = swap_cores(sent)
    o_heads, lse = attend(first, qkv, low)
    o = swap_cores(o_heads)
    hres, atwo, stat = middle(total, x, o, out_w, gain_two, route_w, prev_term, routes[0])
    sent_rows, sent_grads = dispatch(total, experts, cap, flat_t, atwo, dy, stat)
    in_rows = swap_experts(sent_rows).reshape(experts * cap, width)
    in_grads = swap_experts(sent_grads).reshape(experts * cap, width)
    flow, z, a, b = expert_up(in_rows, gate_w, up_w, down_w)
    flow_back = swap_experts(flow.reshape(experts, cap, width)).reshape(experts * cap, width)
    drow, dg, du = expert_down(in_grads, gate_w, up_w, down_w, a, b)
    drow_back = swap_experts(drow.reshape(experts, cap, width)).reshape(experts * cap, width)
    grad_gate, grad_up, grad_down = expert_wgrad(in_rows, in_grads, z, dg, du)

    def scatter_half(grad):
        shape = grad.shape
        share = lax.psum_scatter(
            grad.reshape(2 * shape[1], shape[2]), ("context", "dp"), scatter_dimension=0, tiled=True
        )
        both = lax.all_gather(share, "context", axis=1, tiled=True)
        return both.astype(F32)[None]

    total_gate, total_up, total_down = (
        scatter_half(grad_gate),
        scatter_half(grad_up),
        scatter_half(grad_down),
    )

    output, dh, dolow, dlogit, grad_out_w, small = combine(
        experts,
        total,
        flow_back,
        drow_back,
        flat,
        stat,
        routes[0],
        hres,
        atwo,
        dy,
        o,
        vec,
        gain_two,
        route_w,
        out_w,
    )
    grad_o = swap_cores(dolow)
    grads_sent = attend_back(
        first,
        qkv,
        grad_o,
        o_heads,
        lse,
        low,
        cos.reshape(2, rows, LANES),
        sin.reshape(2, rows, LANES),
    )
    grads = swap_cores(grads_sent)
    grad_tokens, grad_qkv, grad_gain_one = project_back(grads, w_qkv, x, aone, dh, gain_one)

    grad_res = lax.dot_general(
        prev_logits[0],
        dlogit[:, :total],
        (((0,), (0,)), ((), ())),
        precision=HIGH,
        preferred_element_type=F32,
    )
    res_row = jnp.pad(grad_res.reshape(1, -1), ((0, 0), (0, width - total * total)))
    small = jnp.concatenate([small, grad_gain_one, res_row], axis=0)
    small = lax.psum(small, mesh_axes)
    rank = lax.axis_index("dp")
    part = width // dp
    mine = lax.dynamic_slice_in_dim(small, rank * part, part, 1)
    grad_res_total = small[-1, : total * total].reshape(total, total)

    shared = jnp.concatenate([grad_qkv, grad_out_w[None]], axis=0).astype(BF16)
    shared = lax.psum_scatter(shared, "dp", scatter_dimension=1, tiled=True)
    shared = lax.psum(shared, ("expert", "context")).astype(F32)
    return (
        output[None],
        grad_tokens[None],
        mine[-2],
        shared[0],
        shared[1],
        shared[2],
        shared[3],
        mine[total + 4],
        mine[:total].T,
        grad_res_total,
        mine[total : total + 4].T,
        mine[total + 5 : total + 7].T,
        total_gate,
        total_up,
        total_down,
    )


def solution(mesh):
    token = P(("expert", "dp"), "context", None)
    rows = P("dp", None)
    expert = P("expert", "dp", None)
    in_specs = (
        token,
        P(("expert", "dp"), "context"),
        token,
        token,
        token,
        token,
        P("dp"),
        rows,
        rows,
        rows,
        rows,
        P("dp"),
        rows,
        P(),
        rows,
        rows,
        expert,
        expert,
        expert,
    )
    out_specs = (
        token,
        token,
        P("dp"),
        rows,
        rows,
        rows,
        rows,
        P("dp"),
        rows,
        P(),
        rows,
        rows,
        expert,
        expert,
        expert,
    )
    return jax.shard_map(
        on_device, mesh=mesh, in_specs=in_specs, out_specs=out_specs, check_vma=False
    )
```

time: 1720 us -> 761 us (0.44)
  matrix products: 464 us -> 1.56 us
  local copies, waits for them, and re-layouts: 350 us -> 29.4 us
  waiting for transfers between devices: 561 us -> 257 us
  Pallas kernels: 0 us -> 245 us
  other arithmetic: 146 us -> 18.4 us
  blocking collectives: 103 us -> 180 us
  loops' own time: 37.2 us -> 0 us
  starting transfers between devices: 34.2 us -> 9.54 us
    dot_general x62 -> x2, matrix products: 464 us -> 1.56 us  [the longest x1 0.96 us: on_device(): lax.dot_general(prev_logits[0], dlogit[:, :total], (((0,), (0,)), ((), ()...]
    reduce_scatter x7 -> x4, waiting for transfers between devices: 451 us -> 99.2 us  [the longest x3 70.3 us: scatter_half(): lax.psum_scatter(grad.reshape(2 * shape[1], shape[2]), ('context', 'dp'),...]
    pallas_call x0 -> x11, Pallas kernels: none -> 245 us  [the longest x1 61 us: attend_back(): pl.pallas_call(attend_back_kernel, grid_spec=pltpu.PrefetchScalarGridSpec...]
    all_to_all x0 -> x6, blocking collectives: none -> 104 us  [the longest x2 67.1 us: swap_experts(): lax.all_to_all(value, 'expert', split_axis=0, concat_axis=0, tiled=True)]
    reduce_sum x19 -> x1, other arithmetic: 72.6 us -> 1.79 us  [on_device(): starts = jnp.sum((segs[None, :] < segs[:, None]).astype(jnp.int32), axis=1)]
    all_gather x7 -> x5, waiting for transfers between devices: 23.5 us -> 86.9 us  [the longest x1 67 us: on_device(): lax.all_gather(jnp.stack([w_query, w_key, w_value]), 'dp', axis=1, tiled=...]
    dynamic_slice x96 -> x3, local copies, waits for them, and re-layouts: 62.2 us -> 2.37 us  [gather_half(): mine = lax.dynamic_slice_in_dim(shard, core * width, width, 1)]
    unnamed x208 -> x92, local copies, waits for them, and re-layouts: 56.6 us -> 14.1 us
  transfers between devices with their start and end apart: 28 -> 12, of which waited for: 13 -> 6; matrix products, arithmetic and copies ran while one was open for 46% -> 4% of each run, Pallas kernels for 0% -> 27%
where the time goes in v1:
time: 761 us; the launch traced here: 757 us
  waiting for transfers between devices  257 us (34%)
  Pallas kernels  245 us (32%)
  blocking collectives  180 us (24%)
  local copies, waits for them, and re-layouts  29.4 us (4%)
  other arithmetic  18.4 us (2%)
  between operations  14.7 us (2%)
  starting transfers between devices  9.54 us (1%)
    reduce_scatter x3, waiting for transfers between devices, scatter_half(): lax.psum_scatter(grad.reshape(2 * shape[1], shape[2]), ('context', 'dp'),...  70.3 us
    all_to_all x2, blocking collectives, swap_experts(): lax.all_to_all(value, 'expert', split_axis=0, concat_axis=0, tiled=True)  67.1 us
    all_gather x1, waiting for transfers between devices, on_device(): lax.all_gather(jnp.stack([w_query, w_key, w_value]), 'dp', axis=1, tiled=...  67 us
    psum x1, blocking collectives, on_device(): small = lax.psum(small, mesh_axes)  64.3 us
    pallas_call x1, Pallas kernels, attend_back(): pl.pallas_call(attend_back_kernel, grid_spec=pltpu.PrefetchScalarGridSpec...  61 us
    psum x1, waiting for transfers between devices, on_device(): shared = lax.psum(shared, ('expert', 'context')).astype(F32)  53.9 us
    pallas_call x1, Pallas kernels, attend(): pl.pallas_call(attend_kernel, grid_spec=pltpu.PrefetchScalarGridSpec(num_...  48.1 us
    all_to_all x4, blocking collectives, swap_cores(): lax.all_to_all(value, 'context', split_axis=0, concat_axis=0, tiled=True)  36.8 us
  transfers between devices with their start and end apart: 12, of which 6 were waited for; matrix products, arithmetic and copies ran while one was open for 4% of the time, Pallas kernels for 27%

profile of v1, /device:TPU:19, one launch (start us, length us, event | category | flops | bytes accessed | tf_op | source)
XLA Modules:
  0.0 756.7 jit_solution(17827666252742963842)
XLA Ops:
  8.6 2.2 concatenate.13
  12.8 2.2 pad_maximum_fusion.1
  26.9 19.9 %all-gather.7.cloned.1.call-done = bf16[768,896]{1,0:T(8,128)(2,1)} async-done(((bf16[192,896]{1,0:T(8,128)(2,1)}), bf16[768,896]{1,0:T(8,128)(2,1)}) %all-gather.7.cloned.1.call-update) | async-done | bytes 1376272 | tf_op jit(solution)/shard_map/all_gather | solution.py:904
  50.5 67.0 %all-gather.9.cloned.1.call-done.w_ref = bf16[3,768,768]{2,1,0:T(8,128)(2,1)} async-done(((bf16[3,192,768]{2,1,0:T(8,128)(2,1)}), bf16[3,768,768]{2,1,0:T(8,128)(2,1)}) %all-gather.9.cloned.1.call-update) | async-done | bytes 3538960 | tf_op jit(solution)/shard_map/all_gather | solution.py:892
  121.9 5.6 project.1
  128.7 8.1 %all_to_all.40.q_ref.k_ref.v_ref = bf16[2,3,1024,384]{3,2,1,0:T(8,128)(2,1)S(1)} all-to-all(bf16[2,3,1024,384]{3,2,1,0:T(8,128)(2,1)S(1)} %get-tuple-element.46), channel_id=1, replica_groups=mesh['expert'=4,'context'=2,'dp'=4] {'context'}, dimensions={0} | all-to-all | bytes 9437184 | tf_op jit(solution)/shard_map/all_to_all | solution.py:845
  136.8 48.1 %attend.1 = (bf16[2,1024,384]{2,1,0:T(8,128)(2,1)S(1)}, f32[3,8,8,256]{3,2,1,0:T(8,128)S(1)}) custom-call(s32[8]{0:T(128)S(1)} %and_select_fusion.first_ref, bf16[2,3,1024,384]{3,2,1,0:T(8,128)(2,1)S(1)} %all_to_all.40.q_ref.k_ref.v_ref, bf16[2,3,1024,384]{3,2,1,0:T(8,128)(2,1)S(1)} %all_to_all.40.q_ref.k_ref.v_ref, ...), custom_call_target="tpu_custom_call" | custom-call | flops 40000000000 | bytes 6291456 | tf_op jit(solution)/shard_map/attend/pallas_call | solution.py:223
  185.0 5.3 all_to_all.41.o_ref
  191.5 5.5 middle.1
  198.7 4.9 dispatch.1
  203.7 45.2 %all_to_all.42 = bf16[4,288,768]{2,1,0:T(8,128)(2,1)S(1)} all-to-all(bf16[4,288,768]{2,1,0:T(8,128)(2,1)S(1)} %get-tuple-element.50), channel_id=1, replica_groups=mesh['expert'=4,'context'=2,'dp'=4] {'expert'}, dimensions={0} | all-to-all | bytes 3538944 | tf_op jit(solution)/shard_map/all_to_all | solution.py:849
  248.9 4.2 all-to-all-start.4
  253.1 19.9 %expert_up.1 = (bf16[1152,768]{1,0:T(8,128)(2,1)S(1)}, bf16[1152,2048]{1,0:T(8,128)(2,1)}, bf16[1152,2048]{1,0:T(8,128)(2,1)}, bf16[1152,2048]{1,0:T(8,128)(2,1)}) custom-call(bf16[1152,768]{1,0:T(8,128)(2,1)S(1)} %bitcast.64, bf16[2,768,1024]{2,1,0:T(8,128)(2,1)} %bitcast.92, bf16[2,768,1024]{2,1,0:T(8,128)(2,1)} %bitcast.94, bf16[2,2048,384]{2,1,0:T(8,128)(2,1)} %bitcast.90), custom_call_target="tpu_custom_call" | custom-call | flops 10871635968 | bytes 23592960 | tf_op jit(solution)/shard_map/expert_up/pallas_call | solution.py:521
  274.2 26.1 %expert_down.1 = (bf16[1152,768]{1,0:T(8,128)(2,1)}, bf16[1152,2048]{1,0:T(8,128)(2,1)}, bf16[1152,2048]{1,0:T(8,128)(2,1)}) custom-call(bf16[1152,768]{1,0:T(8,128)(2,1)S(1)} %bitcast.66, bf16[2,768,1024]{2,1,0:T(8,128)(2,1)} %bitcast.93, bf16[2,768,1024]{2,1,0:T(8,128)(2,1)} %bitcast.95, bf16[2,2048,384]{2,1,0:T(8,128)(2,1)} %bitcast.91, ...), custom_call_target="tpu_custom_call" | custom-call | flops 10871635968 | bytes 28311552 | tf_op jit(solution)/shard_map/expert_down/pallas_call | solution.py:567
  300.3 16.7 %expert_wgrad.1 = (bf16[2,768,1024]{2,1,0:T(8,128)(2,1)}, bf16[2,768,1024]{2,1,0:T(8,128)(2,1)}, bf16[2,2048,384]{2,1,0:T(8,128)(2,1)}) custom-call(bf16[1152,768]{1,0:T(8,128)(2,1)S(1)} %bitcast.65, bf16[1152,768]{1,0:T(8,128)(2,1)S(1)} %bitcast.67, bf16[1152,2048]{1,0:T(8,128)(2,1)} %get-tuple-element.69.z_ref, ...), custom_call_target="tpu_custom_call" | custom-call | flops 10871635968 | bytes 23592960 | tf_op jit(solution)/shard_map/expert_wgrad/pallas_call | solution.py:604
  318.6 21.9 %all_to_all.43 = bf16[4,288,768]{2,1,0:T(8,128)(2,1)} all-to-all(bf16[4,288,768]{2,1,0:T(8,128)(2,1)S(1)} %bitcast.68), channel_id=1, replica_groups=mesh['expert'=4,'context'=2,'dp'=4] {'expert'}, dimensions={0} | all-to-all | bytes 3538944 | tf_op jit(solution)/shard_map/all_to_all | solution.py:849
  340.4 4.8 all-to-all-start.5
  346.2 16.5 %all-to-all-done.5 = bf16[4,288,768]{2,1,0:T(8,128)(2,1)S(1)} async-done(((bf16[4,288,768]{2,1,0:T(8,128)(2,1)}), bf16[4,288,768]{2,1,0:T(8,128)(2,1)S(1)}, u32[]{:S(2)}, u32[]{:S(2)}) %all-to-all-start.5) | async-done | bytes 1769504 | tf_op jit(solution)/shard_map/all_to_all | solution.py:849
  363.9 34.4 %combine.1 = (bf16[1024,768]{1,0:T(8,128)(2,1)}, f32[1024,768]{1,0:T(8,128)}, bf16[2,1024,384]{2,1,0:T(8,128)(2,1)}, f32[1024,128]{1,0:T(8,128)}, f32[768,768]{1,0:T(8,128)}, /*index=5*/f32[16,768]{1,0:T(8,128)}) custom-call(bf16[1152,768]{1,0:T(8,128)(2,1)} %bitcast.79, bf16[1152,768]{1,0:T(8,128)(2,1)} %bitcast.80, s32[1024,128]{1,0:T(8,128)} %copy-done.22, ...), custom_call_target="tpu_custom_call" | custom-call | flops 7851737088 | bytes 28311552 | tf_op jit(solution)/shard_map/combine/pallas_call | solution.py:736
  398.4 10.6 %all_to_all.44.do_ref = bf16[2,1024,384]{2,1,0:T(8,128)(2,1)S(1)} all-to-all(bf16[2,1024,384]{2,1,0:T(8,128)(2,1)} %get-tuple-element.59), channel_id=1, replica_groups=mesh['expert'=4,'context'=2,'dp'=4] {'context'}, dimensions={0} | all-to-all | bytes 3145728 | tf_op jit(solution)/shard_map/all_to_all | solution.py:845
  409.0 61.0 %attend_back.1 = bf16[2,3,1024,384]{3,2,1,0:T(8,128)(2,1)} custom-call(s32[8]{0:T(128)S(1)} %and_select_fusion.first_ref, bf16[2,3,1024,384]{3,2,1,0:T(8,128)(2,1)} %copy-done.3, bf16[2,3,1024,384]{3,2,1,0:T(8,128)(2,1)} %copy-done.3, bf16[2,3,1024,384]{3,2,1,0:T(8,128)(2,1)} %copy-done.3, bf16[2,1024,384]{2,1,0:T(8,128)(2,1)S(1)} %all_to_all.44.do_ref, ...), custom_call_target="tpu_custom_call" | custom-call | flops 99999997952 | bytes 12582912 | tf_op jit(solution)/shard_map/attend_back/pallas_call | solution.py:349
  470.0 12.8 %all_to_all.45.g_ref = bf16[2,3,1024,384]{3,2,1,0:T(8,128)(2,1)} all-to-all(bf16[2,3,1024,384]{3,2,1,0:T(8,128)(2,1)} %attend_back.1), channel_id=1, replica_groups=mesh['expert'=4,'context'=2,'dp'=4] {'context'}, dimensions={0} | all-to-all | bytes 9437184 | tf_op jit(solution)/shard_map/all_to_all | solution.py:845
  482.8 20.9 %project_back.1 = (f32[1024,768]{1,0:T(8,128)}, f32[3,768,768]{2,1,0:T(8,128)}, f32[1,768]{1,0:T(1,128)}) custom-call(bf16[2,3,1024,384]{3,2,1,0:T(8,128)(2,1)} %all_to_all.45.g_ref, bf16[3,768,768]{2,1,0:T(8,128)(2,1)} %all-gather.9.cloned.1.call-done.w_ref, bf16[1024,768]{1,0:T(8,128)(2,1)} %bitcast.69, bf16[1024,768]{1,0:T(8,128)(2,1)} %copy-done.28, ...), custom_call_target="tpu_custom_call" | custom-call | flops 7247757312 | bytes 26345472 | tf_op jit(solution)/shard_map/project_back/pallas_call | solution.py:817
  503.7 3.5 convert.11
  507.5 2.6 pad_maximum_fusion
  512.3 64.3 %psum.14 = f32[18,768]{1,0:T(8,128)S(1)} all-reduce(f32[18,768]{1,0:T(8,128)S(1)} %select_maximum_fusion), channel_id=1, replica_groups=mesh['expert'=4,'context'=2,'dp'=4] {'expert','context','dp'}, use_global_device_ids=true, to_apply=%region_1.2 | all-reduce | flops 13824 | bytes 110592 | tf_op jit(solution)/shard_map/psum | solution.py:1000
  580.0 4.6 all_gather.38
  584.5 2.6 all_gather.37
  589.7 28.8 %reduce-scatter.5.cloned.1.call-done = bf16[4,192,768]{2,1,0:T(8,128)(2,1)} async-done(((bf16[4,768,768]{2,1,0:T(8,128)(2,1)}), bf16[4,192,768]{2,1,0:T(8,128)(2,1)}) %reduce-scatter.5.cloned.1.call-update) | async-done | bytes 1179664 | tf_op jit(solution)/shard_map/reduce_scatter | solution.py:1007
  618.5 70.3 %reduce-scatter.7.cloned.1.call-done = bf16[192,1024]{1,0:T(8,128)(2,1)} async-done(((bf16[1536,1024]{1,0:T(8,128)(2,1)}), bf16[192,1024]{1,0:T(8,128)(2,1)}) %reduce-scatter.7.cloned.1.call-update) | async-done | bytes 393232 | tf_op jit(solution)/shard_map/reduce_scatter | solution.py:948
  688.9 2.8 all_gather.36
  693.0 53.9 %all-reduce.6.cloned.1.call-done = bf16[4,192,768]{2,1,0:T(8,128)(2,1)} async-done(((bf16[4,192,768]{2,1,0:T(8,128)(2,1)}), bf16[4,192,768]{2,1,0:T(8,128)(2,1)}) %all-reduce.6.cloned.1.call-update) | async-done | bytes 1179664 | tf_op jit(solution)/shard_map/psum | solution.py:1008
  (156 shorter events, 44.8 us)
Async XLA Ops:
  7.2 8.0 %copy-start = (bf16[1,512,768]{2,1,0:T(8,128)(2,1)S(1)}, bf16[1,512,768]{2,1,0:T(8,128)(2,1)}, u32[]{:S(2)}) copy-start(bf16[1,512,768]{2,1,0:T(8,128)(2,1)} %param.39) | copy-start | bytes 2359300
  7.2 39.6 %all-gather.7.cloned.1.call-start = ((), (), s32[]{:S(2)}) async-start(), calls=%async_computation.12 | async-start | bytes 1720320 | tf_op jit(solution)/shard_map/all_gather | solution.py:904
  12.8 104.7 %all-gather.9.cloned.1.call-start = ((), (), s32[]{:S(2)}) async-start(), calls=%async_computation.13 | async-start | bytes 4423680 | tf_op jit(solution)/shard_map/all_gather | solution.py:892
  15.0 6.9 copy-start.41
  15.0 7.2 copy-start.15
  15.1 238.0 %all-gather.15.cloned.1.call-start = ((), (), s32[]{:S(2)}) async-start(), calls=%async_computation.16 | async-start | bytes 3538944 | tf_op jit(solution)/shard_map/all_gather | solution.py:855
  15.1 7.3 copy-start.36
  15.1 7.3 copy-start.44
  16.0 237.1 %all-gather.11.cloned.1.call-start = ((), (), s32[]{:S(2)}) async-start(), calls=%async_computation.14 | async-start | bytes 3538944 | tf_op jit(solution)/shard_map/all_gather | solution.py:855
  16.8 236.3 %all-gather.13.cloned.1.call-start = ((), (), s32[]{:S(2)}) async-start(), calls=%async_computation.15 | async-start | bytes 3538944 | tf_op jit(solution)/shard_map/all_gather | solution.py:855
  22.2 169.3 %copy-start.5 = (s32[1,1024,2]{2,1,0:T(8,128)}, s32[1,1024,2]{2,1,0:T(8,128)S(1)}, u32[]{:S(2)}) copy-start(s32[1,1024,2]{2,1,0:T(8,128)S(1)} %copy.77) | copy-start | bytes 24580
  26.9 90.6 %copy-start.12 = (bf16[1,1024,768]{2,1,0:T(8,128)(2,1)S(1)}, bf16[1,1024,768]{2,1,0:T(8,128)(2,1)}, u32[]{:S(2)}) copy-start(bf16[1,1024,768]{2,1,0:T(8,128)(2,1)} %param.21) | copy-start | bytes 4718596
  47.9 79.6 %copy-start.38 = (f32[768,4]{0,1:T(4,128)}, f32[768,4]{0,1:T(4,128)S(1)}, u32[]{:S(2)}) copy-start(f32[768,4]{0,1:T(4,128)S(1)} %copy.85) | copy-start | bytes 36868
  47.9 79.6 %copy-start.17 = (f32[1,768]{1,0:T(1,128)}, f32[1,768]{1,0:T(1,128)S(1)}, u32[]{:S(2)}) copy-start(f32[1,768]{1,0:T(1,128)S(1)} %get-tuple-element.82.gain_ref) | copy-start | bytes 9220
  47.9 143.6 %copy-start.16 = (f32[1,768]{1,0:T(1,128)}, f32[1,768]{1,0:T(1,128)S(1)}, u32[]{:S(2)}) copy-start(f32[1,768]{1,0:T(1,128)S(1)} %get-tuple-element.81.gain_ref) | copy-start | bytes 9220
  49.0 142.4 %copy-start.14 = (bf16[768,128]{1,0:T(8,128)(2,1)}, bf16[768,128]{1,0:T(8,128)(2,1)S(1)}, u32[]{:S(2)}) copy-start(bf16[768,128]{1,0:T(8,128)(2,1)S(1)} %pad.17.route_ref) | copy-start | bytes 589828
  50.5 141.0 %copy-start.4 = (bf16[768,768]{1,0:T(8,128)(2,1)}, bf16[768,768]{1,0:T(8,128)(2,1)S(1)}, u32[]{:S(2)}) copy-start(bf16[768,768]{1,0:T(8,128)(2,1)S(1)} %slice.78.w_ref) | copy-start | bytes 3538948
  136.8 48.1 %copy-start.3 = (bf16[2,3,1024,384]{3,2,1,0:T(8,128)(2,1)}, bf16[2,3,1024,384]{3,2,1,0:T(8,128)(2,1)S(1)}, u32[]{:S(2)}) copy-start(bf16[2,3,1024,384]{3,2,1,0:T(8,128)(2,1)S(1)} %all_to_all.40.q_ref.k_ref.v_ref) | copy-start | bytes 14155780
  185.0 12.1 %copy-start.29 = (f32[3,8,8,256]{3,2,1,0:T(8,128)}, f32[3,8,8,256]{3,2,1,0:T(8,128)S(1)}, u32[]{:S(2)}) copy-start(f32[3,8,8,256]{3,2,1,0:T(8,128)S(1)} %get-tuple-element.60.lse_ref) | copy-start | bytes 589828
  191.5 7.3 copy-start.20
  203.7 45.2 %copy-start.9 = (bf16[4,288,768]{2,1,0:T(8,128)(2,1)}, bf16[4,288,768]{2,1,0:T(8,128)(2,1)S(1)}, u32[]{:S(2)}) copy-start(bf16[4,288,768]{2,1,0:T(8,128)(2,1)S(1)} %get-tuple-element.52) | copy-start | bytes 5308420
  248.9 25.3 %all-to-all-start.4 = ((bf16[4,288,768]{2,1,0:T(8,128)(2,1)}), bf16[4,288,768]{2,1,0:T(8,128)(2,1)S(1)}, u32[]{:S(2)}, u32[]{:S(2)}) async-start(bf16[4,288,768]{2,1,0:T(8,128)(2,1)} %copy-done.9), calls=%async_computation.4 | async-start | bytes 3538944 | tf_op jit(solution)/shard_map/all_to_all | solution.py:849
  253.1 326.9 %reduce-scatter.11.cloned.1.call-start = ((), (), s32[]{:S(2)}) async-start(), calls=%async_computation.21 | async-start | bytes 3538944 | tf_op jit(solution)/shard_map/reduce_scatter | solution.py:948
  340.4 22.3 %all-to-all-start.5 = ((bf16[4,288,768]{2,1,0:T(8,128)(2,1)}), bf16[4,288,768]{2,1,0:T(8,128)(2,1)S(1)}, u32[]{:S(2)}, u32[]{:S(2)}) async-start(bf16[4,288,768]{2,1,0:T(8,128)(2,1)} %bitcast.20), calls=%async_computation.5 | async-start | bytes 3538944 | tf_op jit(solution)/shard_map/all_to_all | solution.py:849
  345.2 239.3 %reduce-scatter.9.cloned.1.call-start = ((), (), s32[]{:S(2)}) async-start(), calls=%async_computation.20 | async-start | bytes 3538944 | tf_op jit(solution)/shard_map/reduce_scatter | solution.py:948
  345.9 272.6 %reduce-scatter.5.cloned.1.call-start = ((), (), s32[]{:S(2)}) async-start(), calls=%async_computation.17 | async-start | bytes 5898240 | tf_op jit(solution)/shard_map/reduce_scatter | solution.py:1007
  363.9 45.0 %copy-start.25 = (f32[2,1024,128]{2,1,0:T(8,128)S(1)}, f32[2,1024,128]{2,1,0:T(8,128)}, u32[]{:S(2)}) copy-start(f32[2,1024,128]{2,1,0:T(8,128)} %constant.73.cos_ref) | copy-start | bytes 3145732
  398.4 10.6 %copy-start.11 = (bf16[2,1024,384]{2,1,0:T(8,128)(2,1)S(1)}, bf16[2,1024,384]{2,1,0:T(8,128)(2,1)}, u32[]{:S(2)}) copy-start(bf16[2,1024,384]{2,1,0:T(8,128)(2,1)} %copy-done.10) | copy-start | bytes 4718596
  398.4 10.6 %copy-start.24 = (f32[2,1024,128]{2,1,0:T(8,128)S(1)}, f32[2,1024,128]{2,1,0:T(8,128)}, u32[]{:S(2)}) copy-start(f32[2,1024,128]{2,1,0:T(8,128)} %constant.74.sin_ref) | copy-start | bytes 3145732
  398.4 10.6 %copy-start.30 = (f32[3,8,8,256]{3,2,1,0:T(8,128)S(1)}, f32[3,8,8,256]{3,2,1,0:T(8,128)}, u32[]{:S(2)}) copy-start(f32[3,8,8,256]{3,2,1,0:T(8,128)} %copy-done.29) | copy-start | bytes 589828
  510.2 178.7 %reduce-scatter.7.cloned.1.call-start = ((), (), s32[]{:S(2)}) async-start(), calls=%async_computation.19 | async-start | bytes 3538944 | tf_op jit(solution)/shard_map/reduce_scatter | solution.py:948
  510.9 236.0 %all-reduce.6.cloned.1.call-start = ((), (), s32[]{:S(2)}) async-start(), calls=%async_computation.18 | async-start | bytes 2359296 | tf_op jit(solution)/shard_map/psum | solution.py:1008
  (25 other events, 71.4 us)
Sparse Core Ops, SparseCore 0:
  12.9 33.8 all-gather.6
  48.9 68.4 all-gather.8
  119.6 37.5 all-gather.14
  159.3 37.1 all-gather.10
  198.5 37.1 all-gather.12
  317.2 69.5 reduce-scatter.10
  389.1 67.9 reduce-scatter.8
  510.3 108.2 reduce-scatter.4
  620.8 67.9 reduce-scatter.6
  691.9 54.9 all-reduce.5
